TPU v7x, 32 devices: a whole 2x2x4 slice. The times are simulated.
32 devices in a mesh: pipe: 2 (over x), dp: 16 (over z, y, core).
Axes of the slice: x: 2, y: 2, z: 4, core: 2. Of those that a mesh axis runs over, the one named last changes fastest.
Arguments:
- visual_fragments: bfloat16 [2, 16, 64, 1152], P(None, 'dp'), may hold values from -6 to 6
- widening_kernel: bfloat16 [2, 1152, 2176], P('pipe', None, 'dp'), may hold values from -0.1875 to 0.1875
- narrowing_kernel: bfloat16 [2, 2176, 1152], P('pipe', 'dp'), may hold values from -0.125 to 0.125
- caption_outputs: bfloat16 [288, 1152], P(('pipe', 'dp')), may hold values from -6 to 6
- earlier_averaged: float32 [256, 1152], P(('pipe', 'dp')), may hold values from -6 to 6
- match_targets: int32 [288], replicated, may hold values from 0 to 287, each once
- score_scaling: float32 [1], replicated, may hold values from 5 to 15
- score_shift: float32 [1], replicated, may hold values from -4 to -2
Outputs:
- image_grad: float32 [288, 1152], P(('pipe', 'dp'))
- text_grad: float32 [288, 1152], P(('pipe', 'dp'))
Inputs may be any that keep to these rules, and one draw needn't show every extreme that they name: match_targets is a permutation: every text is the positive of exactly one image.
All inputs are finite; a program needn't handle non-finite values.
Results may differ from a plain program's by a relative error of at most 0.017.
Values may be sent and summed in bfloat16 or wider, within the bound.
A program may use at most 128 MiB of HBM per device.

v0:
```python
import jax
import jax.numpy as jnp
from jax import lax
from jax.sharding import PartitionSpec as P


def from_behind(value, axis, steps):
    count = lax.axis_size(axis)
    pairs = [(source, (source + steps) % count) for source in range(count)]
    return lax.ppermute(value, axis, pairs)


def layer_norm(hidden_rows):
    values = hidden_rows.astype(jnp.float32)
    centre = jnp.mean(values, axis=-1, keepdims=True)
    shifted = values - centre
    variance = jnp.mean(shifted * shifted, axis=-1, keepdims=True)
    return (shifted * lax.rsqrt(variance + 1e-06)).astype(jnp.bfloat16)


def section_block(hidden_rows, w_up, w_down):
    normed = layer_norm(hidden_rows)
    pre_act = jnp.dot(normed, w_up, preferred_element_type=jnp.float32)
    activated = jax.nn.gelu(pre_act, approximate=True).astype(jnp.bfloat16)
    updated = hidden_rows.astype(jnp.float32) + jnp.dot(
        activated, w_down, preferred_element_type=jnp.float32
    )
    return updated.astype(jnp.bfloat16)


def unit_rows(values):
    values = values.astype(jnp.float32)
    total = jnp.sum(values * values, axis=-1, keepdims=True)
    return (values * lax.rsqrt(total + 1e-06)).astype(jnp.bfloat16)


def coupling_factors(
    picture_group, source_caption_tile, match_entries, target_tile, sharpness_factor, shift_addend
):
    similarity_scores = (
        sharpness_factor
        * jnp.dot(picture_group, source_caption_tile.T, preferred_element_type=jnp.float32)
        + shift_addend
    )
    matching_couples = match_entries[:, None] == target_tile[None, :]
    coefficient_grid = jnp.where(
        matching_couples,
        -sharpness_factor * jax.nn.sigmoid(-similarity_scores),
        sharpness_factor * jax.nn.sigmoid(similarity_scores),
    )
    return coefficient_grid.astype(jnp.bfloat16)


def body(
    visual_fragments,
    widening_kernel,
    narrowing_kernel,
    caption_outputs,
    earlier_averaged,
    match_targets,
    score_scaling,
    score_shift,
):
    sections = lax.axis_size("pipe")
    section_id = lax.axis_index("pipe")
    data_count = lax.axis_size("dp")
    data_id = lax.axis_index("dp")
    micros, img_mb, patch_count, model_width = visual_fragments.shape
    tok_rows = img_mb * patch_count
    sharpness_factor = score_scaling[0]
    shift_addend = score_shift[0]
    caption_vectors = unit_rows(caption_outputs)
    up_full, down_full = (
        lax.all_gather(widening_kernel, "dp", axis=2, tiled=True),
        lax.all_gather(narrowing_kernel, "dp", axis=1, tiled=True),
    )
    up_full = up_full[0]
    down_full = down_full[0]
    panels = visual_fragments.reshape(micros, tok_rows, model_width)

    def advance(step, current):
        pick = jnp.clip(sections - 1 - step, 0, micros - 1)
        incoming = lax.dynamic_index_in_dim(panels, pick, 0, keepdims=False)
        current = jnp.where((section_id == 0) & (step < sections), incoming, current)
        active = (step >= section_id) & (step - section_id < sections)
        current = lax.cond(
            active,
            lambda carried: section_block(carried, up_full, down_full),
            lambda carried: carried,
            current,
        )
        return from_behind(current, "pipe", 1)

    finished = lax.fori_loop(
        0, 2 * sections - 1, advance, jnp.zeros((tok_rows, model_width), jnp.bfloat16)
    )
    pooled = jnp.mean(
        finished.astype(jnp.float32).reshape(img_mb, patch_count, model_width), axis=1
    )
    picture_vectors = jnp.concatenate([unit_rows(pooled), unit_rows(earlier_averaged)], axis=0)
    rows_dev = picture_vectors.shape[0]
    row_width = data_count * rows_dev
    text_row_block = lax.all_gather(caption_vectors, "dp", axis=0, tiled=True)
    image_column_block = lax.all_gather(picture_vectors, "pipe", axis=0, tiled=True)
    label_table = match_targets.reshape(sections, row_width)
    label_columns = lax.dynamic_slice_in_dim(label_table, data_id * rows_dev, rows_dev, 1).reshape(
        -1
    )
    column_text_block = section_id * row_width + jnp.arange(row_width, dtype=jnp.int32)
    grid_weights = coupling_factors(
        image_column_block,
        text_row_block,
        label_columns,
        column_text_block,
        sharpness_factor,
        shift_addend,
    )
    block = grid_weights
    image_grad = lax.psum_scatter(
        jnp.dot(block, text_row_block, preferred_element_type=jnp.float32).astype(jnp.bfloat16),
        "pipe",
        scatter_dimension=0,
        tiled=True,
    ).astype(jnp.float32)
    block = grid_weights
    text_grad = lax.psum_scatter(
        jnp.dot(block.T, image_column_block, preferred_element_type=jnp.float32),
        "dp",
        scatter_dimension=0,
        tiled=True,
    )
    return (image_grad, text_grad)


def solution(mesh):
    placed = (
        P(None, "dp", None, None),
        P("pipe", None, "dp"),
        P("pipe", "dp", None),
        P(("pipe", "dp"), None),
        P(("pipe", "dp"), None),
        P(),
        P(),
        P(),
    )
    return jax.shard_map(
        body,
        mesh=mesh,
        in_specs=placed,
        out_specs=(P(("pipe", "dp"), None), P(("pipe", "dp"), None)),
        check_vma=False,
    )
```

profile of v0, /device:TPU:1, one launch (start us, length us, event | category | flops | bytes accessed | tf_op | source)
XLA Modules:
  0.0 263.5 jit_solution(2399634407776505768)
XLA Ops:
  8.7 0.8 reshape.74
  9.6 0.9 fusion.34
  10.5 0.8 fusion.36
  11.4 25.6 %all-gather.1 = bf16[16,9,1152]{2,1,0:T(8,128)(2,1)S(1)} all-gather(bf16[1,9,1152]{2,1,0:T(8,128)(2,1)S(1)} %fusion.36), channel_id=1, replica_groups=mesh['pipe'=2,'dp'=16] {'dp'}, dimensions={0}, use_global_device_ids=true | all-gather | bytes 352512 | tf_op jit(solution)/shard_map/all_gather | solution.py:103
  38.5 0.9 multiply_reduce_fusion
  39.4 0.8 multiply_convert_fusion
  40.2 28.6 %all-gather.5.cloned.1.call-done = bf16[1,1152,2176]{1,2,0:T(8,128)(2,1)} async-done(((bf16[1,1152,136]{1,2,0:T(8,128)(2,1)}), bf16[1,1152,2176]{1,2,0:T(8,128)(2,1)}) %all-gather.5.cloned.1.call-update) | async-done | bytes 5013520 | tf_op jit(solution)/shard_map/all_gather | solution.py:74
  68.9 8.4 %copy.12 = bf16[1152,2176]{1,0:T(8,128)(2,1)} copy(bf16[1152,2176]{0,1:T(8,128)(2,1)} %bitcast.29) | data formatting | bytes 10027008 | tf_op jit(solution)/shard_map/while | solution.py:94
  77.3 47.2 %all-gather.7.cloned.1.call-done = bf16[1,2176,1152]{2,1,0:T(8,128)(2,1)} async-done(((bf16[1,136,1152]{2,1,0:T(8,128)(2,1)}), bf16[1,2176,1152]{2,1,0:T(8,128)(2,1)}) %all-gather.7.cloned.1.call-update) | async-done | bytes 5013520 | tf_op jit(solution)/shard_map/all_gather | solution.py:75
  124.6 31.3 %while.14 = (s32[]{:T(128)}, bf16[64,1152]{1,0:T(8,128)(2,1)S(1)}, s32[]{:T(128)}, pred[]{:T(512)}, bf16[2,64,1152]{2,1,0:T(8,128)(2,1)S(1)}, /*index=5*/bf16[11...) while((s32[]{:T(128)}, bf16[64,1152]{1,0:T(8,128)(2,1)S(1)}, ...), condition=%wide.region_5.6_spmd, body=%wide.region_0.5_spmd.sunk | while | flops 644014144 | bytes 11946504 | solution.py:94
  124.6 6.1 %conditional.2 = (bf16[64,1152]{1,0:T(8,128)(2,1)S(1)}) conditional(s32[]{:T(128)} %convert_element_type.108, bf16[64,1152]{1,0:T(8,128)(2,1)S(1)} %bitcast_select_fusion.2, (bf16[64,1152]{1,0:T(8,128)(2,1)S(1)}, bf16[1152,2176]{1,0:T(8,128)(2,1)}, bf16[2176,1152]{1,0:T(8,128)(2,1)}) %tuple.49), branch_computations={%region_1.1_spmd, %region_2.4_spmd} | conditional | flops 643940416 | bytes 10914056 | solution.py:86
  125.0 5.7 %fusion.1 = bf16[64,1152]{1,0:T(8,128)(2,1)S(1)} fusion(bf16[2176,1152]{1,0:T(8,128)(2,1)} %get-tuple-element.146, bf16[64,1152]{1,0:T(8,128)(2,1)S(1)} %copy.25, bf16[1152,2176]{1,0:T(8,128)(2,1)} %get-tuple-element.145, f32[64]{0:T(128)S(1)} %add_rsqrt_fusion, f32[64]{0:T(128)S(1)} %broadcast_multiply_fusion), kind=kOutput, calls=%fused_computation.1 | convolution fusion | flops 643497984 | bytes 10322432 | tf_op jit(solution)/shard_map/while/body/eval_jaxpr/cond/branch_1_fun/dot_general | solution.py:25
  130.8 5.2 %collective-permute-done = bf16[64,1152]{1,0:T(8,128)(2,1)S(1)} collective-permute-done((bf16[64,1152]{1,0:T(8,128)(2,1)S(1)}, bf16[64,1152]{1,0:T(8,128)(2,1)S(1)}, u32[]{:S(2)}, u32[]{:S(2)}) %collective-permute-start) | collective-permute-done | bytes 147488 | tf_op jit(solution)/shard_map/while/body/eval_jaxpr/ppermute | solution.py:10
  136.0 6.1 %conditional.2 = (bf16[64,1152]{1,0:T(8,128)(2,1)S(1)}) conditional(s32[]{:T(128)} %convert_element_type.108, bf16[64,1152]{1,0:T(8,128)(2,1)S(1)} %bitcast_select_fusion.2, (bf16[64,1152]{1,0:T(8,128)(2,1)S(1)}, bf16[1152,2176]{1,0:T(8,128)(2,1)}, bf16[2176,1152]{1,0:T(8,128)(2,1)}) %tuple.49), branch_computations={%region_1.1_spmd, %region_2.4_spmd} | conditional | flops 643940416 | bytes 10914056 | solution.py:86
  136.4 5.7 %fusion.1 = bf16[64,1152]{1,0:T(8,128)(2,1)S(1)} fusion(bf16[2176,1152]{1,0:T(8,128)(2,1)} %get-tuple-element.146, bf16[64,1152]{1,0:T(8,128)(2,1)S(1)} %copy.25, bf16[1152,2176]{1,0:T(8,128)(2,1)} %get-tuple-element.145, f32[64]{0:T(128)S(1)} %add_rsqrt_fusion, f32[64]{0:T(128)S(1)} %broadcast_multiply_fusion), kind=kOutput, calls=%fused_computation.1 | convolution fusion | flops 643497984 | bytes 10322432 | tf_op jit(solution)/shard_map/while/body/eval_jaxpr/cond/branch_1_fun/dot_general | solution.py:25
  142.5 3.7 %collective-permute-done = bf16[64,1152]{1,0:T(8,128)(2,1)S(1)} collective-permute-done((bf16[64,1152]{1,0:T(8,128)(2,1)S(1)}, bf16[64,1152]{1,0:T(8,128)(2,1)S(1)}, u32[]{:S(2)}, u32[]{:S(2)}) %collective-permute-start) | collective-permute-done | bytes 147488 | tf_op jit(solution)/shard_map/while/body/eval_jaxpr/ppermute | solution.py:10
  146.2 7.1 %collective-permute-start = (bf16[64,1152]{1,0:T(8,128)(2,1)S(1)}, bf16[64,1152]{1,0:T(8,128)(2,1)S(1)}, u32[]{:S(2)}, u32[]{:S(2)}) collective-permute-start(bf16[64,1152]{1,0:T(8,128)(2,1)S(1)} %get-tuple-element.253), channel_id=1, source_target_pairs={{0,16},{16,0},{1,17},{17,1},{2,18},{18,2},{3,19},{19,3},{4,20},{20... | collective-permute-start | bytes 442376 | tf_op jit(solution)/shard_map/while/body/eval_jaxpr/ppermute | solution.py:10
  153.3 2.5 collective-permute-done
  157.2 3.5 %all-gather = bf16[2,9,1152]{2,1,0:T(8,128)(2,1)S(1)} all-gather(bf16[1,9,1152]{2,1,0:T(8,128)(2,1)S(1)} %maximum_bitcast_fusion), channel_id=1, replica_groups=mesh['pipe'=2,'dp'=16] {'pipe'}, dimensions={0}, use_global_device_ids=true | all-gather | bytes 62208 | tf_op jit(solution)/shard_map/all_gather | solution.py:104
  161.0 1.2 fusion.37
  162.4 5.8 %fusion = bf16[16,1152]{1,0:T(8,128)(2,1)S(1)} fusion(bf16[18,1152]{1,0:T(8,128)(2,1)S(1)} %convolution_convert_fusion), kind=kCustom, calls=%all-reduce-scatter | all-reduce-scatter fusion | flops 36865 | bytes 78848
  168.2 1.9 collective-permute-start.1
  173.5 81.9 %all-reduce.5.cloned.1.call-done = f32[144,1152]{1,0:T(8,128)} async-done(((f32[144,1152]{1,0:T(8,128)}), f32[144,1152]{1,0:T(8,128)}) %all-reduce.5.cloned.1.call-update) | async-done | bytes 663568
  255.4 1.5 constant_dynamic-slice_fusion
  (49 shorter events, 6.3 us)
Async XLA Ops:
  7.2 61.7 %all-gather.5.cloned.1.call-start = ((), (), s32[]{:S(2)}) async-start(), calls=%async_computation | async-start | bytes 5326848 | tf_op jit(solution)/shard_map/all_gather | solution.py:74
  7.9 116.6 %all-gather.7.cloned.1.call-start = ((), (), s32[]{:S(2)}) async-start(), calls=%async_computation.1 | async-start | bytes 5326848 | tf_op jit(solution)/shard_map/all_gather | solution.py:75
  8.6 246.8 %all-reduce.5.cloned.1.call-start = ((), (), s32[]{:S(2)}) async-start(), calls=%async_computation.2 | async-start | bytes 1327104
  68.9 55.7 %copy-start = (bf16[2,1,64,1152]{3,2,1,0:T(8,128)(2,1)S(1)}, bf16[2,1,64,1152]{3,2,1,0:T(8,128)(2,1)}, u32[]{:S(2)}) copy-start(bf16[2,1,64,1152]{3,2,1,0:T(8,128)(2,1)} %param.12) | copy-start | bytes 884740
  124.5 45.6 %copy-start.1 = (u32[32]{0:T(128)S(1)}, u32[32]{0:T(128)}, u32[]{:S(2)}) copy-start(u32[32]{0:T(128)} %constant.87) | copy-start | bytes 388
  124.6 46.8 %copy-start.2 = (u32[32]{0:T(128)S(1)}, u32[32]{0:T(128)}, u32[]{:S(2)}) copy-start(u32[32]{0:T(128)} %constant.91) | copy-start | bytes 388
  130.7 5.3 %collective-permute-start = (bf16[64,1152]{1,0:T(8,128)(2,1)S(1)}, bf16[64,1152]{1,0:T(8,128)(2,1)S(1)}, u32[]{:S(2)}, u32[]{:S(2)}) collective-permute-start(bf16[64,1152]{1,0:T(8,128)(2,1)S(1)} %get-tuple-element.253), channel_id=1, source_target_pairs={{0,16},{16,0},{1,17},{17,1},{2,18},{18,2},{3,19},{19,3},{4,20},{20... | collective-permute-start | bytes 442376 | tf_op jit(solution)/shard_map/while/body/eval_jaxpr/ppermute | solution.py:10
  142.1 4.1 %collective-permute-start = (bf16[64,1152]{1,0:T(8,128)(2,1)S(1)}, bf16[64,1152]{1,0:T(8,128)(2,1)S(1)}, u32[]{:S(2)}, u32[]{:S(2)}) collective-permute-start(bf16[64,1152]{1,0:T(8,128)(2,1)S(1)} %get-tuple-element.253), channel_id=1, source_target_pairs={{0,16},{16,0},{1,17},{17,1},{2,18},{18,2},{3,19},{19,3},{4,20},{20... | collective-permute-start | bytes 442376 | tf_op jit(solution)/shard_map/while/body/eval_jaxpr/ppermute | solution.py:10
  146.2 9.6 %collective-permute-start = (bf16[64,1152]{1,0:T(8,128)(2,1)S(1)}, bf16[64,1152]{1,0:T(8,128)(2,1)S(1)}, u32[]{:S(2)}, u32[]{:S(2)}) collective-permute-start(bf16[64,1152]{1,0:T(8,128)(2,1)S(1)} %get-tuple-element.253), channel_id=1, source_target_pairs={{0,16},{16,0},{1,17},{17,1},{2,18},{18,2},{3,19},{19,3},{4,20},{20... | collective-permute-start | bytes 442376 | tf_op jit(solution)/shard_map/while/body/eval_jaxpr/ppermute | solution.py:10
  168.2 4.4 %collective-permute-start.1 = (bf16[7,1152]{1,0:T(8,128)(2,1)S(1)}, bf16[7,1152]{1,0:T(8,128)(2,1)S(1)}, u32[]{:S(2)}, u32[]{:S(2)}) collective-permute-start(bf16[7,1152]{1,0:T(8,128)(2,1)S(1)} %slice), channel_id=1, source_target_pairs={{0,16},{1,17},{2,18},{3,19},{4,20},{5,21},{6,22},{7,23},{8,24},{9,... | collective-permute-start | bytes 48392
Sparse Core Ops, SparseCore 0:
  10.1 58.6 all-gather.4
  71.0 53.4 all-gather.6
  162.3 93.0 all-reduce.4
where the time goes:
time: 265 us; the launch traced here: 263 us
  waiting for transfers between devices  171 us (65%)
  blocking collectives  34.9 us (13%)
  between operations  17.2 us (6%)
  matrix products  13 us (5%)
  local copies, waits for them, and re-layouts  12.5 us (5%)
  starting transfers between devices  9.6 us (4%)
  other arithmetic  5.56 us (2%)
    unnamed x5, waiting for transfers between devices  83.3 us
    all_gather x1, waiting for transfers between devices, body(): lax.all_gather(narrowing_kernel, 'dp', axis=1, tiled=True)  47.2 us
    all_gather x1, waiting for transfers between devices, body(): lax.all_gather(widening_kernel, 'dp', axis=2, tiled=True)  28.6 us
    all_gather x1, blocking collectives, body(): text_row_block = lax.all_gather(caption_vectors, 'dp', axis=0, tiled=True)  25.6 us
    dot_general x2, matrix products, section_block(): jnp.dot(activated, w_down, preferred_element_type=jnp.float32)  11.4 us
    ppermute x3, waiting for transfers between devices, from_behind(): return lax.ppermute(value, axis, pairs)  11.4 us
    while x1, local copies, waits for them, and re-layouts, body(): lax.fori_loop(0, 2 * sections - 1, advance, jnp.zeros((tok_rows, model_wi...  8.45 us
    ppermute x3, starting transfers between devices, from_behind(): return lax.ppermute(value, axis, pairs)  7.57 us
  transfers between devices with their start and end apart: 7, of which 6 were waited for; matrix products, arithmetic and copies ran while one was open for 8% of the time, Pallas kernels for 0%

commit v1 on v0

v1 whole, which is shorter than its diff:
```python
import functools

import jax
import jax.numpy as jnp
from jax import lax
from jax.experimental import pallas as pl
from jax.experimental.pallas import tpu as pltpu
from jax.sharding import PartitionSpec as P

F32, BF16 = jnp.float32, jnp.bfloat16
SLOT = 32
MID = 16
TILE = 256
NT = (((1,), (1,)), ((), ()))
NN = (((1,), (0,)), ((), ()))


def dot(a, b, dims):
    return lax.dot_general(a, b, dims, preferred_element_type=F32)


def layer_norm(values):
    shifted = values - jnp.mean(values, axis=-1, keepdims=True)
    variance = jnp.mean(shifted * shifted, axis=-1, keepdims=True)
    return (shifted * lax.rsqrt(variance + 1e-06)).astype(BF16)


def unit_rows(values):
    total = jnp.sum(values * values, axis=-1, keepdims=True)
    return (values * lax.rsqrt(total + 1e-06)).astype(BF16)


def kernel(
    cfg,
    scale_ref, shift_ref, ids_ref, tids_ref, x_ref, w_ref, cap_ref, prior_ref,
    img_ref, txt_ref, *rest,
):
    n_pipe, n_dp, micros, rows, width, ff, texts, priors, spill = cfg
    if spill:
        eg, *rest = rest
    else:
        *rest, eg = rest
    (own, chunk, ug, dg, xg, part, sc, rc, sz, rz, ma, ma2, mx, mx2, tp, tall,
     w_s, w_r, x_s, x_r, c_s, c_r, z_s, z_r, h_s, h_r, tp_s, tp_r, ta_s, ta_r,
     ez_s, ez_r, ey_s, ey_r, ex_s, ex_r, ec_s, ec_r, loc) = rest
    p, d = lax.axis_index("pipe"), lax.axis_index("dp")
    c, y, z = d % 2, (d // 2) % 2, d // 4
    zb, zp = z % 2, z // 2
    nz = n_dp // 4
    nzp = nz // 2
    groups = 2 * nzp
    last = n_pipe - 1
    oc, oz = 1 - c, 1 - zb

    def at(z_, y_, c_):
        return (z_ * 2 + y_) * 2 + c_

    d_c, d_y, d_z = at(z, y, oc), at(z, 1 - y, c), at(zp * 2 + oz, y, c)

    def copy(src, dst, s, r, pipe, dp):
        return pltpu.make_async_remote_copy(
            src_ref=src, dst_ref=dst, send_sem=s, recv_sem=r,
            device_id=(pipe, dp), device_id_type=pl.DeviceIdType.MESH)

    def arrived(dst, r):
        copy(dst, dst, loc.at[0], r, p, d_c).wait_recv()

    def left(src, s):
        copy(src, src, s, loc.at[0], p, d_c).wait_send()

    barrier = pltpu.get_barrier_semaphore()
    total = n_pipe * n_dp

    def greet(i, _):
        t = (p * n_dp + d + i) % total
        pl.semaphore_signal(barrier, inc=1, device_id=(t // n_dp, t % n_dp),
                            device_id_type=pl.DeviceIdType.MESH)
        return 0

    lax.fori_loop(1, total, greet, 0)

    own[...] = jnp.zeros_like(own)
    own[0:texts, :] = unit_rows(cap_ref[...].astype(F32))
    own[MID:MID + priors, :] = unit_rows(prior_ref[...])

    @pl.when(p == 0)
    def _():
        for m in range(micros):
            xg[zb, m, c] = x_ref[m]

    q = zp * 2 + y

    def wslot(ref, q_):
        return ref.at[pl.ds(pl.multiple_of(q_ * ff, 16), ff), :]

    for k, ref in enumerate((ug, dg)):
        ref[pl.ds(pl.multiple_of(q * ff, 16), ff), :] = w_ref[k]
    pl.semaphore_wait(barrier, total - 1)

    big = ((0, ug), (1, dg))

    def w_own_y(k, ref):
        return copy(w_ref.at[k], wslot(ref, q), w_s.at[k, 0], w_r.at[k, q], p, d_y)

    def w_own_z(k, ref, i):
        t = at(((zp + i) % nzp) * 2 + zb, y, c)
        return copy(w_ref.at[k], wslot(ref, q), w_s.at[k, i], w_r.at[k, q], p, t)

    def w_fwd(k, ref, i):
        q_ = ((zp + i) % nzp) * 2 + y
        return copy(wslot(ref, q_), wslot(ref, q_), w_s.at[k, nzp + i], w_r.at[k, q_], p, d_y)

    def x_c(m):
        return copy(xg.at[zb, m, c], xg.at[zb, m, c], x_s.at[0, m], x_r.at[zb, m, c], p, d_c)

    def x_z(m):
        return copy(xg.at[zb, m, c], xg.at[zb, m, c], x_s.at[1, m], x_r.at[zb, m, c], p, d_z)

    def x_f(m):
        return copy(xg.at[oz, m, c], xg.at[oz, m, c], x_s.at[2, m], x_r.at[oz, m, c], p, d_c)

    for k, ref in big:
        for i in range(1, nzp):
            w_own_z(k, ref, i).start()
        w_own_y(k, ref).start()
        if k == 0:
            @pl.when(p == 0)
            def _():
                for m in range(micros):
                    x_c(m).start()
                    x_z(m).start()

    def eslot(index, count):
        return eg.at[pl.ds(index, count)]

    e_own = ((c * n_pipe + p) * 2 + y) * nz + z
    e_y, e_x, e_c = ((c * n_pipe + p) * 2 + y) * nz, (c * n_pipe + p) * 2 * nz, c * n_pipe * 2 * nz

    def e_z(i):
        t = (z + i) % nz
        return copy(own, eg.at[e_own], ez_s.at[i], ez_r.at[z], p, at(t, y, c))

    for i in range(1, nz):
        e_z(i).start()
    keep = pltpu.make_async_copy(own, eg.at[e_own], loc.at[1])
    keep.start()

    for k, ref in big:
        for i in range(1, nzp):
            q_ = ((zp + i) % nzp) * 2 + y
            arrived(wslot(ref, q_), w_r.at[k, q_])
            w_fwd(k, ref, i).start()

    keep.wait()
    for i in range(1, nz):
        t = (z + i) % nz
        arrived(eg.at[e_y + t], ez_r.at[t])
    send_y = copy(eslot(e_y, nz), eslot(e_y, nz), ey_s, ey_r, p, d_y)
    send_y.start()

    def tokens_on():
        for m in range(micros):
            arrived(xg.at[oz, m, c], x_r.at[oz, m, c])
            x_f(m).start()

    def tokens_here():
        for m in range(micros):
            arrived(xg.at[zb, m, oc], x_r.at[zb, m, oc])
            arrived(xg.at[oz, m, oc], x_r.at[oz, m, oc])

    @pl.when(p == 0)
    def _():
        tokens_on()

    e_yo = ((c * n_pipe + p) * 2 + 1 - y) * nz
    arrived(eslot(e_yo, nz), ey_r)

    def e_xs(i):
        return copy(eslot(e_x, 2 * nz), eslot(e_x, 2 * nz), ex_s.at[i], ex_r.at[p],
                    (p + i) % n_pipe, d)

    for i in range(1, n_pipe):
        e_xs(i).start()

    for k, ref in big:
        for i in range(nzp):
            q_ = ((zp + i) % nzp) * 2 + 1 - y
            arrived(wslot(ref, q_), w_r.at[k, q_])

    def emb_finish():
        for i in range(1, n_pipe):
            t = (p + i) % n_pipe
            arrived(eslot((c * n_pipe + t) * 2 * nz, 2 * nz), ex_r.at[t])
        send_c = copy(eslot(e_c, n_pipe * 2 * nz), eslot(e_c, n_pipe * 2 * nz), ec_s, ec_r, p, d_c)
        send_c.start()
        arrived(eslot(oc * n_pipe * 2 * nz, n_pipe * 2 * nz), ec_r)
        send_c.wait_send()

    span = micros * 2 * rows
    tile = min(TILE, span)
    tiles = span // tile
    per = tile // rows
    mt = per // 2

    def activate(b, j):
        values = xg[b, pl.ds(j * mt, mt)].reshape(tile, width).astype(F32)
        act = jax.nn.gelu(dot(layer_norm(values), ug[...], NT), approximate=True)
        return values, act.astype(BF16)

    def hidden_out(m):
        return copy(sz.at[1, m], xg.at[zb, m, c], h_s.at[m], h_r.at[m],
                    jnp.minimum(p + 1, last), d)

    def to_core(b, m):
        return copy(sc.at[b, m], rc.at[b, m], c_s.at[b, m], c_r.at[b, m], p, d_c)

    def to_z(m):
        return copy(sz.at[0, m], rz.at[m], z_s.at[m], z_r.at[m], p, d_z)

    @pl.when(p > 0)
    def _():
        emb_finish()
        for m in range(micros):
            arrived(xg.at[zb, m, c], h_r.at[m])
            x_c(m).start()
            x_z(m).start()
        tokens_on()

    tokens_here()

    @pl.when(p < last)
    def _():
        for b in (oz, zb):
            def step(j, _, b=b):
                _, act = activate(b, j)
                out = dot(act, dg[...], NN)
                part[b, pl.ds(j * mt, mt)] = out.reshape(mt, 2, rows, width)
                return 0

            lax.fori_loop(0, tiles, step, 0)
            for m in range(micros):
                sc[b, m] = part[b, m, oc].astype(BF16)
                to_core(b, m).start()
            if b is oz:
                for m in range(micros):
                    arrived(rc.at[oz, m], c_r.at[oz, m])
                    sz[0, m] = (part[oz, m, c] + rc[oz, m].astype(F32)).astype(BF16)
                    to_z(m).start()
        for m in range(micros):
            arrived(rc.at[zb, m], c_r.at[zb, m])
            arrived(rz.at[m], z_r.at[m])
            new = part[zb, m, c] + rc[zb, m].astype(F32) + rz[m].astype(F32)
            sz[1, m] = (new + xg[zb, m, c].astype(F32)).astype(BF16)
            hidden_out(m).start()
        for m in range(micros):
            for b in range(2):
                left(sc.at[b, m], c_s.at[b, m])
            left(sz.at[0, m], z_s.at[m])
            left(sz.at[1, m], h_s.at[m])

    @pl.when(p == 0)
    def _():
        emb_finish()

    scale, shift = scale_ref[0], shift_ref[0]
    n_rows = total * SLOT
    cs = chunk.shape[0] if spill else n_rows
    ids_w = ids_ref.shape[1]

    def column(ref, first, count, limit):
        lane = lax.broadcasted_iota(jnp.int32, (count, limit), 1)
        row = lax.broadcasted_iota(jnp.int32, (count, limit), 0)
        return jnp.max(jnp.where(lane == row + first, ref[...], -1), axis=1, keepdims=True)

    def weigh(scores, row_ids, col_ids, keep_mask):
        logits = scale * scores + shift
        positive = row_ids == col_ids
        w = jnp.where(positive, -scale * jax.nn.sigmoid(-logits), scale * jax.nn.sigmoid(logits))
        return jnp.where(keep_mask, w, 0.0).astype(BF16)

    def block(j):
        if not spill:
            return eg[...].reshape(n_rows, width), ids_ref[...]
        fetch = pltpu.make_async_copy(eg.at[pl.ds(j * (cs // SLOT), cs // SLOT)], chunk2, loc.at[1])
        fetch.start()
        fetch.wait()
        return chunk2[...].reshape(cs, width), ids_ref[:, pl.ds(pl.multiple_of(j * cs, cs), cs)]

    chunk2 = chunk.reshape(cs // SLOT, SLOT, width) if spill else None
    own_v = own[...]
    own_ids = column(ids_ref, e_own * SLOT, SLOT, ids_w)
    kind_r = lax.broadcasted_iota(jnp.int32, (SLOT, cs), 0)
    kind_c = lax.broadcasted_iota(jnp.int32, (SLOT, cs), 1) % SLOT
    text_c = kind_c < texts
    prior_c = (kind_c >= MID) & (kind_c < MID + priors)
    mask = ((kind_r < texts) & prior_c) | ((kind_r >= MID) & text_c)

    def early(j, acc):
        e, ids = block(j)
        w = weigh(dot(own_v, e, NT), own_ids, ids, mask)
        return acc + dot(w, e, NN)

    if spill:
        grads = lax.fori_loop(0, n_rows // cs, early, jnp.zeros((SLOT, width), F32))
    else:
        grads = early(0, 0.0)
    img_ref[1:1 + priors, :] = grads[MID:MID + priors]

    @pl.when(p == last)
    def _():
        def step(i, _):
            b, j = i // tiles, i % tiles
            values, act = activate(b, j)
            ma[i] = jnp.mean(act.astype(F32).reshape(per, rows, -1), axis=1)
            mx[i] = jnp.mean(values.reshape(per, rows, width), axis=1)
            return 0

        lax.fori_loop(0, 2 * tiles, step, 0)
        for i in range(2 * tiles):
            ma2[i * per:(i + 1) * per, :] = ma[i]
            mx2[i * per:(i + 1) * per, :] = mx[i]
        t = zb * 2 + c
        tp[t] = dot(ma2[...].astype(BF16), dg[...], NN)

        def t_out(i):
            t_ = (t + i) % 4
            return copy(tp.at[t], tp.at[t], tp_s.at[i], tp_r.at[t], p,
                        at(zp * 2 + t_ // 2, y, t_ % 2))

        for i in range(1, 4):
            t_out(i).start()
        for i in range(1, 4):
            t_ = (t + i) % 4
            arrived(tp.at[t_], tp_r.at[t_])
        pooled = mx2[...] + (tp[0] + tp[1]) + (tp[2] + tp[3])
        tall[q] = unit_rows(pooled).astype(F32)

        def spread(i, _):
            s = (last * groups + q + i) % (n_pipe * groups)
            g = s % groups
            copy(tall.at[q], tall.at[q], ta_s.at[i], ta_r.at[q], s // groups,
                 at((g // 2) * 2 + zb, g % 2, c)).start()
            return 0

        lax.fori_loop(1, n_pipe * groups, spread, 0)
        for i in range(1, 4):
            left(tp.at[t], tp_s.at[i])
        for i in range(1, groups):
            g = (q + i) % groups
            arrived(tall.at[g], ta_r.at[g])
        for i in range(1, n_pipe * groups):
            left(tall.at[q], ta_s.at[i])

    @pl.when(p != last)
    def _():
        for g in range(groups):
            arrived(tall.at[g], ta_r.at[g])

    n_t = tall.shape[0] * tall.shape[1]
    towers = tall[...].reshape(n_t, width).astype(BF16)
    t_ids = tids_ref[...][:, :n_t]
    rmask = lax.broadcasted_iota(jnp.int32, (SLOT, n_t), 0) < texts
    w = weigh(dot(own_v, towers, NT), own_ids, t_ids, rmask)
    txt_ref[...] = (grads + dot(w, towers, NN))[:texts]

    mine = (zb * micros + p) * 2 + c
    pick = lax.broadcasted_iota(jnp.int32, (tall.shape[1], width), 0) == mine
    row = jnp.sum(jnp.where(pick, tall[q], 0.0), axis=0, keepdims=True)
    row8 = jnp.broadcast_to(row, (8, width)).astype(BF16)
    row_id = column(tids_ref, q * tall.shape[1] + mine, 1, tids_ref.shape[1])
    row_ids = jnp.broadcast_to(row_id, (8, 1))

    def late(j, acc):
        e, ids = block(j)
        w = weigh(dot(row8, e, NT), row_ids, ids, text_c[:8])
        return acc + dot(w, e, NN)

    if spill:
        g_row = lax.fori_loop(0, n_rows // cs, late, jnp.zeros((8, width), F32))
    else:
        g_row = late(0, 0.0)
    img_ref[0:1, :] = g_row[0:1]

    for k, ref in big:
        for i in range(nzp):
            left(w_ref.at[k], w_s.at[k, i])
        for i in range(1, nzp):
            left(w_ref.at[k], w_s.at[k, nzp + i])
    for m in range(micros):
        for i in range(3):
            left(xg.at[zb, m, c], x_s.at[i, m])
    for i in range(1, nz):
        left(own, ez_s.at[i])
    send_y.wait_send()
    for i in range(1, n_pipe):
        left(eslot(e_x, 2 * nz), ex_s.at[i])


def body(vis, up, down, cap, prior, match, scale, shift):
    n_pipe, n_dp = lax.axis_size("pipe"), lax.axis_size("dp")
    micros, img_mb, patch, width = vis.shape
    rows = img_mb * patch
    shard = up.shape[2]
    ff = -(-shard // 16) * 16
    texts, priors = cap.shape[0], prior.shape[0]
    nz, total = n_dp // 4, n_pipe * n_dp
    nzp = nz // 2
    groups = 2 * nzp
    w = jnp.stack([up[0].T, down[0]])
    w = jnp.pad(w, ((0, 0), (0, ff - shard), (0, 0)))
    per = texts
    table = match.reshape(n_pipe, nz, 2, 2, per).transpose(3, 0, 2, 1, 4).reshape(total, per)
    own_text = jnp.arange(total * texts, dtype=jnp.int32).reshape(n_pipe, nz, 2, 2, texts)
    own_text = own_text.transpose(3, 0, 2, 1, 4).reshape(total, texts)
    ids = jnp.concatenate([
        jnp.pad(own_text, ((0, 0), (0, MID - texts)), constant_values=-2),
        jnp.pad(table[:, 1:], ((0, 0), (0, SLOT - MID - priors)), constant_values=-2),
    ], axis=1).reshape(1, total * SLOT)
    tids = match.reshape(micros, nzp, 2, 2, 2, per)[..., 0].transpose(1, 3, 2, 0, 4).reshape(1, -1)
    n_t = tids.shape[1]
    tids = jnp.pad(tids, ((0, 0), (0, -n_t % 128)), constant_values=-2)
    spill = total > 64
    cfg = (n_pipe, n_dp, micros, rows, width, ff, texts, priors, spill)
    span = micros * 2 * rows
    tile = min(TILE, span)
    tiles, kept = span // tile, tile // rows
    imgs = 4 * micros
    ffg = groups * ff
    vm = pl.BlockSpec(memory_space=pltpu.VMEM)
    sm = pl.BlockSpec(memory_space=pltpu.SMEM)
    dma = pltpu.SemaphoreType.DMA
    outs = [jax.ShapeDtypeStruct((texts, width), F32)] * 2
    out_specs = [vm, vm]
    eg_shape = (total, SLOT, width)
    scratch = [
        pltpu.VMEM((SLOT, width), BF16),
        pltpu.VMEM((1024, width) if spill else (16, width), BF16),
        pltpu.VMEM((ffg, width), BF16),
        pltpu.VMEM((ffg, width), BF16),
        pltpu.VMEM((2, micros, 2, rows, width), BF16),
        pltpu.VMEM((2, micros, 2, rows, width), F32),
        pltpu.VMEM((2, micros, rows, width), BF16),
        pltpu.VMEM((2, micros, rows, width), BF16),
        pltpu.VMEM((2, micros, rows, width), BF16),
        pltpu.VMEM((micros, rows, width), BF16),
        pltpu.VMEM((2 * tiles, kept, ffg), F32),
        pltpu.VMEM((imgs, ffg), F32),
        pltpu.VMEM((2 * tiles, kept, width), F32),
        pltpu.VMEM((imgs, width), F32),
        pltpu.VMEM((4, imgs, width), F32),
        pltpu.VMEM((groups, imgs, width), F32),
        dma((2, 2 * nzp)), dma((2, groups)),
        dma((3, micros)), dma((2, micros, 2)),
        dma((2, micros)), dma((2, micros)),
        dma((micros,)), dma((micros,)),
        dma((micros,)), dma((micros,)),
        dma((4,)), dma((4,)),
        dma((n_pipe * groups,)), dma((groups,)),
        dma((nz,)), dma((nz,)),
        dma, dma,
        dma((n_pipe,)), dma((n_pipe,)),
        dma, dma,
        dma((2,)),
    ]
    if spill:
        outs = outs + [jax.ShapeDtypeStruct(eg_shape, BF16)]
        out_specs = out_specs + [pl.BlockSpec(memory_space=pl.ANY)]
    else:
        scratch = scratch + [pltpu.VMEM(eg_shape, BF16)]
    result = pl.pallas_call(
        functools.partial(kernel, cfg),
        out_shape=outs,
        in_specs=[sm, sm, vm, vm, vm, vm, vm, vm],
        out_specs=out_specs,
        scratch_shapes=scratch,
        compiler_params=pltpu.CompilerParams(
            collective_id=0, has_side_effects=True, vmem_limit_bytes=60 * 2**20),
    )(scale, shift, ids, tids, vis.reshape(micros, rows, width), w, cap, prior)
    return result[0], result[1]


def solution(mesh):
    placed = (
        P(None, "dp", None, None),
        P("pipe", None, "dp"),
        P("pipe", "dp", None),
        P(("pipe", "dp"), None),
        P(("pipe", "dp"), None),
        P(),
        P(),
        P(),
    )
    return jax.shard_map(
        body,
        mesh=mesh,
        in_specs=placed,
        out_specs=(P(("pipe", "dp"), None), P(("pipe", "dp"), None)),
        check_vma=False,
    )
```

time: 265 us -> 111 us (0.42)
  the two profiles are of different devices: /device:TPU:1 before, /device:TPU:11 now
where the time goes in v1:
time: 111 us
  Pallas kernels  99.9 us (90%)
  local copies, waits for them, and re-layouts  6.73 us (6%)
  other arithmetic  2.12 us (2%)
  between operations  1.98 us (2%)
    pallas_call x1, Pallas kernels, body(): pl.pallas_call(functools.partial(kernel, cfg), out_shape=outs, in_specs=[...  99.9 us
    unnamed x2, local copies, waits for them, and re-layouts  3.04 us

profile of v1, /device:TPU:11, one launch (start us, length us, event | category | flops | bytes accessed | tf_op | source)
XLA Modules:
  0.0 110.7 jit_solution(4918441088746259283)
XLA Ops:
  1.9 0.1 reshape.71
  2.0 0.1 reshape.75
  2.1 0.1 reshape.79
  2.2 0.1 reshape.83
  2.3 0.1 add_add_fusion
  2.4 0.8 reshape.88
  3.2 0.4 slice_reduce_fusion
  3.6 0.1 reshape.89
  3.7 0.5 pad.18.tids_ref
  4.2 0.8 reshape.85
  5.0 0.1 slice.8
  5.1 0.1 select_add_fusion
  5.2 0.7 reshape.87.ids_ref
  5.8 1.9 %fusion.2.w_ref = bf16[2,144,1152]{2,1,0:T(8,128)(2,1)} fusion(bf16[1,136,1152]{2,1,0:T(8,128)(2,1)} %param.10, bf16[1,136,1152]{2,1,0:T(8,128)(2,1)} %bitcast.9), kind=kLoop, calls=%fused_computation.3 | loop fusion | flops 2322432 | bytes 1290240 | tf_op jit(solution)/shard_map/stack | solution.py:409
  7.8 99.9 %shard_map.95 = (f32[9,1152]{1,0:T(8,128)}, f32[9,1152]{1,0:T(8,128)}) custom-call(f32[1]{0:T(128)S(6)} %copy.16.scale_ref, f32[1]{0:T(128)S(6)} %copy.17.shift_ref, s32[1,1024]{1,0:T(1,128)} %reshape.87.ids_ref, s32[1,128]{1,0:T(1,128)} %pad.18.tids_ref, bf16[2,64,1152]{2,1,0:T(8,128)(2,1)} %bitcast.10, bf16[2,144,1152]{2,1,0:T(8,128)(2,1)} %fusion.2.w_ref, ...), custom_call_target="tpu_custom_call" | custom-call | tf_op jit(solution)/shard_map/pallas_call | solution.py:470
  107.7 1.5 %copy.18 = f32[9,1152]{1,0:T(8,128)} copy(f32[9,1152]{1,0:T(8,128)} %get-tuple-element.4) | data formatting | bytes 82944
  109.2 1.5 %copy.19 = f32[9,1152]{1,0:T(8,128)} copy(f32[9,1152]{1,0:T(8,128)} %get-tuple-element.5) | data formatting | bytes 82944
  (6 shorter events, 0.0 us)

commit v2 on v1

--- a/solution.py
+++ b/solution.py
@@ -32,7 +32,7 @@
 
 def kernel(
     cfg,
-    scale_ref, shift_ref, ids_ref, tids_ref, x_ref, w_ref, cap_ref, prior_ref,
+    scale_ref, shift_ref, ids_ref, tids_ref, x_ref, up_ref, down_ref, cap_ref, prior_ref,
     img_ref, txt_ref, *rest,
 ):
     n_pipe, n_dp, micros, rows, width, ff, texts, priors, spill = cfg
@@ -40,9 +40,9 @@
         eg, *rest = rest
     else:
         *rest, eg = rest
-    (own, chunk, ug, dg, xg, part, sc, rc, sz, rz, ma, ma2, mx, mx2, tp, tall,
+    (own, chunk, w_ref, ug, dg, xg, part, sc, rc, sz, rz, ma, ma2, mx, mx2, tp, tall,
      w_s, w_r, x_s, x_r, c_s, c_r, z_s, z_r, h_s, h_r, tp_s, tp_r, ta_s, ta_r,
-     ez_s, ez_r, ey_s, ey_r, ex_s, ex_r, ec_s, ec_r, loc) = rest
+     ea_s, ea_r, ez_s, ez_r, ey_s, ey_r, ex_s, ex_r, ec_s, ec_r, loc) = rest
     p, d = lax.axis_index("pipe"), lax.axis_index("dp")
     c, y, z = d % 2, (d // 2) % 2, d // 4
     zb, zp = z % 2, z // 2
@@ -93,7 +93,11 @@
     def wslot(ref, q_):
         return ref.at[pl.ds(pl.multiple_of(q_ * ff, 16), ff), :]
 
-    for k, ref in enumerate((ug, dg)):
+    shard = up_ref.shape[0]
+    for k, (ref, given) in enumerate(((ug, up_ref), (dg, down_ref))):
+        w_ref[k, 0:shard, :] = given[...]
+        if ff > shard:
+            w_ref[k, shard:ff, :] = jnp.zeros((ff - shard, width), BF16)
         ref[pl.ds(pl.multiple_of(q * ff, 16), ff), :] = w_ref[k]
     pl.semaphore_wait(barrier, total - 1)
 
@@ -119,82 +123,119 @@
     def x_f(m):
         return copy(xg.at[oz, m, c], xg.at[oz, m, c], x_s.at[2, m], x_r.at[oz, m, c], p, d_c)
 
-    for k, ref in big:
+    def w_start(k, ref):
         for i in range(1, nzp):
             w_own_z(k, ref, i).start()
         w_own_y(k, ref).start()
-        if k == 0:
-            @pl.when(p == 0)
-            def _():
-                for m in range(micros):
-                    x_c(m).start()
-                    x_z(m).start()
-
-    def eslot(index, count):
-        return eg.at[pl.ds(index, count)]
-
-    e_own = ((c * n_pipe + p) * 2 + y) * nz + z
-    e_y, e_x, e_c = ((c * n_pipe + p) * 2 + y) * nz, (c * n_pipe + p) * 2 * nz, c * n_pipe * 2 * nz
-
-    def e_z(i):
-        t = (z + i) % nz
-        return copy(own, eg.at[e_own], ez_s.at[i], ez_r.at[z], p, at(t, y, c))
-
-    for i in range(1, nz):
-        e_z(i).start()
-    keep = pltpu.make_async_copy(own, eg.at[e_own], loc.at[1])
-    keep.start()
-
-    for k, ref in big:
+
+    def w_on(k, ref):
         for i in range(1, nzp):
             q_ = ((zp + i) % nzp) * 2 + y
             arrived(wslot(ref, q_), w_r.at[k, q_])
             w_fwd(k, ref, i).start()
 
-    keep.wait()
-    for i in range(1, nz):
-        t = (z + i) % nz
-        arrived(eg.at[e_y + t], ez_r.at[t])
-    send_y = copy(eslot(e_y, nz), eslot(e_y, nz), ey_s, ey_r, p, d_y)
-    send_y.start()
-
-    def tokens_on():
-        for m in range(micros):
-            arrived(xg.at[oz, m, c], x_r.at[oz, m, c])
-            x_f(m).start()
-
-    def tokens_here():
-        for m in range(micros):
-            arrived(xg.at[zb, m, oc], x_r.at[zb, m, oc])
-            arrived(xg.at[oz, m, oc], x_r.at[oz, m, oc])
-
-    @pl.when(p == 0)
-    def _():
-        tokens_on()
-
-    e_yo = ((c * n_pipe + p) * 2 + 1 - y) * nz
-    arrived(eslot(e_yo, nz), ey_r)
-
-    def e_xs(i):
-        return copy(eslot(e_x, 2 * nz), eslot(e_x, 2 * nz), ex_s.at[i], ex_r.at[p],
-                    (p + i) % n_pipe, d)
-
-    for i in range(1, n_pipe):
-        e_xs(i).start()
-
-    for k, ref in big:
+    def w_here(k, ref):
         for i in range(nzp):
             q_ = ((zp + i) % nzp) * 2 + 1 - y
             arrived(wslot(ref, q_), w_r.at[k, q_])
 
-    def emb_finish():
+    def eslot(index, count):
+        return eg.at[pl.ds(index, count)]
+
+    e_own = ((c * 2 + y) * nz + z) * n_pipe + p
+    e_z, e_y, e_c = ((c * 2 + y) * nz + z) * n_pipe, (c * 2 + y) * nz * n_pipe, c * 2 * nz * n_pipe
+    many = 2 * nz * n_pipe
+    send_a = copy(own, eg.at[e_own], ea_s, ea_r.at[p], last, d)
+    send_y = copy(eslot(e_y, nz * n_pipe), eslot(e_y, nz * n_pipe), ey_s, ey_r, p, d_y)
+    send_c = copy(eslot(e_c, many), eslot(e_c, many), ec_s, ec_r, p, d_c)
+
+    def send_z(i):
+        return copy(eslot(e_z, n_pipe), eslot(e_z, n_pipe), ez_s.at[i], ez_r.at[z], p,
+                    at((z + i) % nz, y, c))
+
+    def send_x(i):
+        return copy(eslot(e_c, many), eslot(e_c, many), ex_s.at[i], ex_r, (p + i) % n_pipe, d)
+
+    def tokens_on():
+        for m in range(micros):
+            arrived(xg.at[oz, m, c], x_r.at[oz, m, c])
+            x_f(m).start()
+
+    def tokens_here():
+        for m in range(micros):
+            arrived(xg.at[zb, m, oc], x_r.at[zb, m, oc])
+            arrived(xg.at[oz, m, oc], x_r.at[oz, m, oc])
+
+    w_start(0, ug)
+
+    @pl.when(p == 0)
+    def _():
+        for m in range(micros):
+            x_c(m).start()
+            x_z(m).start()
+
+    @pl.when(p != last)
+    def _():
+        send_a.start()
+        w_start(1, dg)
+        w_on(0, ug)
+
+    @pl.when(p == 0)
+    def _():
+        tokens_on()
+
+    @pl.when(p == last)
+    def _():
+        keep = pltpu.make_async_copy(own, eg.at[e_own], loc.at[1])
+        keep.start()
+        keep.wait()
+        for t in range(last):
+            arrived(eg.at[e_z + t], ea_r.at[t])
+        for i in range(1, nz):
+            send_z(i).start()
+        w_on(0, ug)
+        w_start(1, dg)
+        for i in range(1, nz):
+            t = (z + i) % nz
+            arrived(eslot(e_y + t * n_pipe, n_pipe), ez_r.at[t])
+        send_y.start()
+        w_on(1, dg)
+        arrived(eslot((c * 2 + 1 - y) * nz * n_pipe, nz * n_pipe), ey_r)
+        send_c.start()
         for i in range(1, n_pipe):
-            t = (p + i) % n_pipe
-            arrived(eslot((c * n_pipe + t) * 2 * nz, 2 * nz), ex_r.at[t])
-        send_c = copy(eslot(e_c, n_pipe * 2 * nz), eslot(e_c, n_pipe * 2 * nz), ec_s, ec_r, p, d_c)
-        send_c.start()
-        arrived(eslot(oc * n_pipe * 2 * nz, n_pipe * 2 * nz), ec_r)
-        send_c.wait_send()
+            send_x(i).start()
+        w_here(0, ug)
+        arrived(eslot(oc * many, many), ec_r)
+
+    @pl.when(p != last)
+    def _():
+        w_on(1, dg)
+        w_here(0, ug)
+
+    if spill:
+        ids_all, tids_all = ids_ref, tids_ref
+    else:
+        count = ids_ref.shape[1]
+        square = (lax.broadcasted_iota(jnp.int32, (count, count), 0)
+                  == lax.broadcasted_iota(jnp.int32, (count, count), 1))
+        matches = jnp.max(jnp.where(square, ids_ref[...], -1), axis=1, keepdims=True)
+
+        def look_up(index):
+            shape = (count, index.shape[1])
+            hit = lax.broadcasted_iota(jnp.int32, shape, 0) == index
+            return jnp.max(jnp.where(hit, matches, -2), axis=0, keepdims=True)
+
+        lane = lax.broadcasted_iota(jnp.int32, (1, total * SLOT), 1)
+        s, r = lane // SLOT, lane % SLOT
+        unit = s // n_pipe
+        home = (s % n_pipe) * n_dp + ((unit % nz) * 2 + (unit // nz) % 2) * 2 + unit // (2 * nz)
+        images = jnp.where((r >= MID) & (r < MID + priors), home * texts + 1 + r - MID, -1)
+        ids_all = jnp.where(r < texts, home * texts + r, look_up(images))
+        lane = lax.broadcasted_iota(jnp.int32, (1, 128), 1)
+        m_, b_ = (lane // 2) % micros, (lane // (2 * micros)) % 2
+        y_, z_ = (lane // (4 * micros)) % 2, lane // (8 * micros)
+        home = m_ * n_dp + ((z_ * 2 + b_) * 2 + y_) * 2 + lane % 2
+        tids_all = look_up(jnp.where(lane < tall.shape[0] * tall.shape[1], home * texts, -1))
 
     span = micros * 2 * rows
     tile = min(TILE, span)
@@ -217,27 +258,35 @@
     def to_z(m):
         return copy(sz.at[0, m], rz.at[m], z_s.at[m], z_r.at[m], p, d_z)
 
-    @pl.when(p > 0)
-    def _():
-        emb_finish()
+    def take_hidden():
         for m in range(micros):
             arrived(xg.at[zb, m, c], h_r.at[m])
             x_c(m).start()
             x_z(m).start()
         tokens_on()
 
-    tokens_here()
+    @pl.when((p > 0) & (p < last))
+    def _():
+        take_hidden()
 
     @pl.when(p < last)
     def _():
+        tokens_here()
+        if tiles > 1:
+            w_here(1, dg)
         for b in (oz, zb):
             def step(j, _, b=b):
                 _, act = activate(b, j)
+                if b is oz and tiles == 1:
+                    w_here(1, dg)
                 out = dot(act, dg[...], NN)
                 part[b, pl.ds(j * mt, mt)] = out.reshape(mt, 2, rows, width)
                 return 0
 
-            lax.fori_loop(0, tiles, step, 0)
+            if tiles == 1:
+                step(0, 0)
+            else:
+                lax.fori_loop(0, tiles, step, 0)
             for m in range(micros):
                 sc[b, m] = part[b, m, oc].astype(BF16)
                 to_core(b, m).start()
@@ -258,14 +307,14 @@
             left(sz.at[0, m], z_s.at[m])
             left(sz.at[1, m], h_s.at[m])
 
-    @pl.when(p == 0)
-    def _():
-        emb_finish()
+        arrived(eslot(e_c, many), ex_r)
+        send_c.start()
+        arrived(eslot(oc * many, many), ec_r)
 
     scale, shift = scale_ref[0], shift_ref[0]
     n_rows = total * SLOT
     cs = chunk.shape[0] if spill else n_rows
-    ids_w = ids_ref.shape[1]
+    ids_w = n_rows
 
     def column(ref, first, count, limit):
         lane = lax.broadcasted_iota(jnp.int32, (count, limit), 1)
@@ -280,15 +329,15 @@
 
     def block(j):
         if not spill:
-            return eg[...].reshape(n_rows, width), ids_ref[...]
+            return eg[...].reshape(n_rows, width), ids_all
         fetch = pltpu.make_async_copy(eg.at[pl.ds(j * (cs // SLOT), cs // SLOT)], chunk2, loc.at[1])
         fetch.start()
         fetch.wait()
-        return chunk2[...].reshape(cs, width), ids_ref[:, pl.ds(pl.multiple_of(j * cs, cs), cs)]
+        return chunk2[...].reshape(cs, width), ids_all[:, pl.ds(pl.multiple_of(j * cs, cs), cs)]
 
     chunk2 = chunk.reshape(cs // SLOT, SLOT, width) if spill else None
     own_v = own[...]
-    own_ids = column(ids_ref, e_own * SLOT, SLOT, ids_w)
+    own_ids = column(ids_all, e_own * SLOT, SLOT, ids_w)
     kind_r = lax.broadcasted_iota(jnp.int32, (SLOT, cs), 0)
     kind_c = lax.broadcasted_iota(jnp.int32, (SLOT, cs), 1) % SLOT
     text_c = kind_c < texts
@@ -315,7 +364,10 @@
             mx[i] = jnp.mean(values.reshape(per, rows, width), axis=1)
             return 0
 
+        take_hidden()
+        tokens_here()
         lax.fori_loop(0, 2 * tiles, step, 0)
+        w_here(1, dg)
         for i in range(2 * tiles):
             ma2[i * per:(i + 1) * per, :] = ma[i]
             mx2[i * per:(i + 1) * per, :] = mx[i]
@@ -358,7 +410,7 @@
 
     n_t = tall.shape[0] * tall.shape[1]
     towers = tall[...].reshape(n_t, width).astype(BF16)
-    t_ids = tids_ref[...][:, :n_t]
+    t_ids = tids_all[...][:, :n_t]
     rmask = lax.broadcasted_iota(jnp.int32, (SLOT, n_t), 0) < texts
     w = weigh(dot(own_v, towers, NT), own_ids, t_ids, rmask)
     txt_ref[...] = (grads + dot(w, towers, NN))[:texts]
@@ -367,7 +419,7 @@
     pick = lax.broadcasted_iota(jnp.int32, (tall.shape[1], width), 0) == mine
     row = jnp.sum(jnp.where(pick, tall[q], 0.0), axis=0, keepdims=True)
     row8 = jnp.broadcast_to(row, (8, width)).astype(BF16)
-    row_id = column(tids_ref, q * tall.shape[1] + mine, 1, tids_ref.shape[1])
+    row_id = column(tids_all, q * tall.shape[1] + mine, 1, tids_all.shape[1])
     row_ids = jnp.broadcast_to(row_id, (8, 1))
 
     def late(j, acc):
@@ -389,11 +441,37 @@
     for m in range(micros):
         for i in range(3):
             left(xg.at[zb, m, c], x_s.at[i, m])
-    for i in range(1, nz):
-        left(own, ez_s.at[i])
-    send_y.wait_send()
-    for i in range(1, n_pipe):
-        left(eslot(e_x, 2 * nz), ex_s.at[i])
+    send_c.wait_send()
+
+    @pl.when(p == last)
+    def _():
+        for i in range(1, nz):
+            left(eslot(e_z, n_pipe), ez_s.at[i])
+        send_y.wait_send()
+        for i in range(1, n_pipe):
+            left(eslot(e_c, many), ex_s.at[i])
+
+    @pl.when(p != last)
+    def _():
+        send_a.wait_send()
+
+
+def id_rows(match, n_pipe, nz, texts, priors):
+    total = n_pipe * nz * 4
+
+    def placed(numbers):
+        numbers = numbers.reshape(n_pipe, nz, 2, 2, texts)
+        return numbers.transpose(3, 2, 1, 0, 4).reshape(total, texts)
+
+    ids = jnp.concatenate([
+        jnp.pad(placed(jnp.arange(total * texts, dtype=jnp.int32)),
+                ((0, 0), (0, MID - texts)), constant_values=-2),
+        jnp.pad(placed(match)[:, 1:], ((0, 0), (0, SLOT - MID - priors)), constant_values=-2),
+    ], axis=1).reshape(1, total * SLOT)
+    tids = match.reshape(n_pipe, nz // 2, 2, 2, 2, texts)[..., 0]
+    tids = tids.transpose(1, 3, 2, 0, 4).reshape(1, -1)
+    tids = jnp.pad(tids, ((0, 0), (0, -tids.shape[1] % 128)), constant_values=-2)
+    return ids, tids
 
 
 def body(vis, up, down, cap, prior, match, scale, shift):
@@ -406,20 +484,11 @@
     nz, total = n_dp // 4, n_pipe * n_dp
     nzp = nz // 2
     groups = 2 * nzp
-    w = jnp.stack([up[0].T, down[0]])
-    w = jnp.pad(w, ((0, 0), (0, ff - shard), (0, 0)))
-    per = texts
-    table = match.reshape(n_pipe, nz, 2, 2, per).transpose(3, 0, 2, 1, 4).reshape(total, per)
-    own_text = jnp.arange(total * texts, dtype=jnp.int32).reshape(n_pipe, nz, 2, 2, texts)
-    own_text = own_text.transpose(3, 0, 2, 1, 4).reshape(total, texts)
-    ids = jnp.concatenate([
-        jnp.pad(own_text, ((0, 0), (0, MID - texts)), constant_values=-2),
-        jnp.pad(table[:, 1:], ((0, 0), (0, SLOT - MID - priors)), constant_values=-2),
-    ], axis=1).reshape(1, total * SLOT)
-    tids = match.reshape(micros, nzp, 2, 2, 2, per)[..., 0].transpose(1, 3, 2, 0, 4).reshape(1, -1)
-    n_t = tids.shape[1]
-    tids = jnp.pad(tids, ((0, 0), (0, -n_t % 128)), constant_values=-2)
     spill = total > 64
+    if spill:
+        ids, tids = id_rows(match, n_pipe, nz, texts, priors)
+    else:
+        ids = tids = match.reshape(1, -1)
     cfg = (n_pipe, n_dp, micros, rows, width, ff, texts, priors, spill)
     span = micros * 2 * rows
     tile = min(TILE, span)
@@ -435,6 +504,7 @@
     scratch = [
         pltpu.VMEM((SLOT, width), BF16),
         pltpu.VMEM((1024, width) if spill else (16, width), BF16),
+        pltpu.VMEM((2, ff, width), BF16),
         pltpu.VMEM((ffg, width), BF16),
         pltpu.VMEM((ffg, width), BF16),
         pltpu.VMEM((2, micros, 2, rows, width), BF16),
@@ -456,9 +526,10 @@
         dma((micros,)), dma((micros,)),
         dma((4,)), dma((4,)),
         dma((n_pipe * groups,)), dma((groups,)),
+        dma, dma((n_pipe,)),
         dma((nz,)), dma((nz,)),
         dma, dma,
-        dma((n_pipe,)), dma((n_pipe,)),
+        dma((n_pipe,)), dma,
         dma, dma,
         dma((2,)),
     ]
@@ -470,12 +541,12 @@
     result = pl.pallas_call(
         functools.partial(kernel, cfg),
         out_shape=outs,
-        in_specs=[sm, sm, vm, vm, vm, vm, vm, vm],
+        in_specs=[sm, sm, vm, vm, vm, vm, vm, vm, vm],
         out_specs=out_specs,
         scratch_shapes=scratch,
         compiler_params=pltpu.CompilerParams(
             collective_id=0, has_side_effects=True, vmem_limit_bytes=60 * 2**20),
-    )(scale, shift, ids, tids, vis.reshape(micros, rows, width), w, cap, prior)
+    )(scale, shift, ids, tids, vis.reshape(micros, rows, width), up[0].T, down[0], cap, prior)
     return result[0], result[1]
 
 

time: 111 us -> 99.1 us (0.89)
  the two profiles are of different devices: /device:TPU:11 before, /device:TPU:1 now
where the time goes in v2:
time: 99.1 us; the launch traced here: 98.8 us
  Pallas kernels  93.5 us (94%)
  local copies, waits for them, and re-layouts  3.43 us (3%)
  between operations  1.95 us (2%)
    pallas_call x1, Pallas kernels, body(): pl.pallas_call(functools.partial(kernel, cfg), out_shape=outs, in_specs=[...  93.5 us
    unnamed x6, local copies, waits for them, and re-layouts  2.87 us

profile of v2, /device:TPU:1, one launch (start us, length us, event | category | flops | bytes accessed | tf_op | source)
XLA Modules:
  0.0 98.8 jit_solution(9956954151972273128)
XLA Ops:
  1.9 0.0 copy-start.1
  1.9 0.7 copy-done.1
  2.6 0.6 reshape.10.ids_ref.tids_ref
  3.2 93.5 %shard_map.95 = (f32[9,1152]{1,0:T(8,128)}, f32[9,1152]{1,0:T(8,128)}) custom-call(f32[1]{0:T(128)S(6)} %copy.12.scale_ref, f32[1]{0:T(128)S(6)} %copy.13.shift_ref, s32[1,288]{1,0:T(1,128)} %reshape.10.ids_ref.tids_ref, s32[1,288]{1,0:T(1,128)} %reshape.10.ids_ref.tids_ref, bf16[2,64,1152]{2,1,0:T(8,128)(2,1)} %bitcast.7, bf16[136,1152]{1,0:T(8,128)(2,1)} %bitcast.5, ...), custom_call_target="tpu_custom_call" | custom-call | tf_op jit(solution)/shard_map/pallas_call | solution.py:541
  96.6 0.0 copy-start
  96.7 1.6 %copy.14 = f32[9,1152]{1,0:T(8,128)} copy(f32[9,1152]{1,0:T(8,128)} %get-tuple-element.4) | data formatting | bytes 82944
  98.2 0.0 copy-done
  98.2 0.6 copy.15
Async XLA Ops:
  1.9 0.7 copy-start.1
  96.6 1.6 %copy-start = (f32[9,1152]{1,0:T(8,128)S(1)}, f32[9,1152]{1,0:T(8,128)}, u32[]{:S(2)}) copy-start(f32[9,1152]{1,0:T(8,128)} %get-tuple-element.5) | copy-start | bytes 124420

commit v3 on v2

--- a/solution.py
+++ b/solution.py
@@ -40,9 +40,10 @@
         eg, *rest = rest
     else:
         *rest, eg = rest
-    (own, chunk, w_ref, ug, dg, xg, part, sc, rc, sz, rz, ma, ma2, mx, mx2, tp, tall,
+    (own, chunk, w_ref, ul, dl, xl, rx, ug, dg, xg, part, sc, rc, sz, rz, ma, ma2, mx, mx2, tp, tall,
      w_s, w_r, x_s, x_r, c_s, c_r, z_s, z_r, h_s, h_r, tp_s, tp_r, ta_s, ta_r,
-     ea_s, ea_r, ez_s, ez_r, ey_s, ey_r, ex_s, ex_r, ec_s, ec_r, loc) = rest
+     ea_s, ea_r, ez_s, ez_r, ey_s, ey_r, ex_s, ex_r, ec_s, ec_r,
+     hw_s, hw_r, hx_s, hx_r, xl_s, xl_r, loc) = rest
     p, d = lax.axis_index("pipe"), lax.axis_index("dp")
     c, y, z = d % 2, (d // 2) % 2, d // 4
     zb, zp = z % 2, z // 2
@@ -83,10 +84,10 @@
     own[0:texts, :] = unit_rows(cap_ref[...].astype(F32))
     own[MID:MID + priors, :] = unit_rows(prior_ref[...])
 
-    @pl.when(p == 0)
-    def _():
-        for m in range(micros):
-            xg[zb, m, c] = x_ref[m]
+    @pl.when(p <= 1)
+    def _():
+        for m in range(micros):
+            xl[zb, m, c] = x_ref[m]
 
     q = zp * 2 + y
 
@@ -94,34 +95,65 @@
         return ref.at[pl.ds(pl.multiple_of(q_ * ff, 16), ff), :]
 
     shard = up_ref.shape[0]
+    half = ul.shape[0] // groups
     for k, (ref, given) in enumerate(((ug, up_ref), (dg, down_ref))):
         w_ref[k, 0:shard, :] = given[...]
-        if ff > shard:
-            w_ref[k, shard:ff, :] = jnp.zeros((ff - shard, width), BF16)
-        ref[pl.ds(pl.multiple_of(q * ff, 16), ff), :] = w_ref[k]
+        if 2 * half > shard:
+            w_ref[k, shard:2 * half, :] = jnp.zeros((2 * half - shard, width), BF16)
+        ref[pl.ds(pl.multiple_of(q * ff, 16), ff), :] = w_ref[k, 0:ff, :]
+
+    @pl.when(p == 0)
+    def _():
+        for k, ref in enumerate((ul, dl)):
+            ref[pl.ds(pl.multiple_of(q * half, 16), half), :] = w_ref[k, 0:half, :]
     pl.semaphore_wait(barrier, total - 1)
 
     big = ((0, ug), (1, dg))
 
     def w_own_y(k, ref):
-        return copy(w_ref.at[k], wslot(ref, q), w_s.at[k, 0], w_r.at[k, q], p, d_y)
+        return copy(w_ref.at[k, pl.ds(0, ff)], wslot(ref, q), w_s.at[k, 0], w_r.at[k, q], p, d_y)
 
     def w_own_z(k, ref, i):
         t = at(((zp + i) % nzp) * 2 + zb, y, c)
-        return copy(w_ref.at[k], wslot(ref, q), w_s.at[k, i], w_r.at[k, q], p, t)
+        return copy(w_ref.at[k, pl.ds(0, ff)], wslot(ref, q), w_s.at[k, i], w_r.at[k, q], p, t)
 
     def w_fwd(k, ref, i):
         q_ = ((zp + i) % nzp) * 2 + y
         return copy(wslot(ref, q_), wslot(ref, q_), w_s.at[k, nzp + i], w_r.at[k, q_], p, d_y)
 
-    def x_c(m):
-        return copy(xg.at[zb, m, c], xg.at[zb, m, c], x_s.at[0, m], x_r.at[zb, m, c], p, d_c)
-
-    def x_z(m):
-        return copy(xg.at[zb, m, c], xg.at[zb, m, c], x_s.at[1, m], x_r.at[zb, m, c], p, d_z)
-
-    def x_f(m):
-        return copy(xg.at[oz, m, c], xg.at[oz, m, c], x_s.at[2, m], x_r.at[oz, m, c], p, d_c)
+    def x_c(buf, ss, rr, m):
+        return copy(buf.at[zb, m, c], buf.at[zb, m, c], ss.at[0, m], rr.at[zb, m, c], p, d_c)
+
+    def x_z(buf, ss, rr, m):
+        return copy(buf.at[zb, m, c], buf.at[zb, m, c], ss.at[1, m], rr.at[zb, m, c], p, d_z)
+
+    def x_f(buf, ss, rr, m):
+        return copy(buf.at[oz, m, c], buf.at[oz, m, c], ss.at[2, m], rr.at[oz, m, c], p, d_c)
+
+    def hslot(ref, q_):
+        return ref.at[pl.ds(pl.multiple_of(q_ * half, 16), half), :]
+
+    halves = ((0, ul), (1, dl))
+
+    def h_over(k, ref):
+        return copy(w_ref.at[k, pl.ds(half, half)], hslot(ref, q), hx_s.at[k], hx_r.at[k], 1, d)
+
+    def h_start(k, ref):
+        for i in range(1, nzp):
+            t = at(((zp + i) % nzp) * 2 + zb, y, c)
+            copy(hslot(ref, q), hslot(ref, q), hw_s.at[k, i], hw_r.at[k, q], p, t).start()
+        copy(hslot(ref, q), hslot(ref, q), hw_s.at[k, 0], hw_r.at[k, q], p, d_y).start()
+
+    def h_on(k, ref):
+        for i in range(1, nzp):
+            q_ = ((zp + i) % nzp) * 2 + y
+            arrived(hslot(ref, q_), hw_r.at[k, q_])
+            copy(hslot(ref, q_), hslot(ref, q_), hw_s.at[k, nzp + i], hw_r.at[k, q_], p, d_y).start()
+
+    def h_here(k, ref):
+        for i in range(nzp):
+            q_ = ((zp + i) % nzp) * 2 + 1 - y
+            arrived(hslot(ref, q_), hw_r.at[k, q_])
 
     def w_start(k, ref):
         for i in range(1, nzp):
@@ -156,36 +188,21 @@
     def send_x(i):
         return copy(eslot(e_c, many), eslot(e_c, many), ex_s.at[i], ex_r, (p + i) % n_pipe, d)
 
-    def tokens_on():
-        for m in range(micros):
-            arrived(xg.at[oz, m, c], x_r.at[oz, m, c])
-            x_f(m).start()
-
-    def tokens_here():
-        for m in range(micros):
-            arrived(xg.at[zb, m, oc], x_r.at[zb, m, oc])
-            arrived(xg.at[oz, m, oc], x_r.at[oz, m, oc])
-
-    w_start(0, ug)
-
-    @pl.when(p == 0)
-    def _():
-        for m in range(micros):
-            x_c(m).start()
-            x_z(m).start()
-
-    @pl.when(p != last)
-    def _():
-        send_a.start()
-        w_start(1, dg)
-        w_on(0, ug)
-
-    @pl.when(p == 0)
-    def _():
-        tokens_on()
-
-    @pl.when(p == last)
-    def _():
+    def tokens_out(buf, ss, rr, m):
+        x_c(buf, ss, rr, m).start()
+        x_z(buf, ss, rr, m).start()
+
+    def tokens_on(buf, ss, rr):
+        for m in range(micros):
+            arrived(buf.at[oz, m, c], rr.at[oz, m, c])
+            x_f(buf, ss, rr, m).start()
+
+    def tokens_here(buf, rr):
+        for m in range(micros):
+            arrived(buf.at[zb, m, oc], rr.at[zb, m, oc])
+            arrived(buf.at[oz, m, oc], rr.at[oz, m, oc])
+
+    def emb_start():
         keep = pltpu.make_async_copy(own, eg.at[e_own], loc.at[1])
         keep.start()
         keep.wait()
@@ -193,24 +210,59 @@
             arrived(eg.at[e_z + t], ea_r.at[t])
         for i in range(1, nz):
             send_z(i).start()
-        w_on(0, ug)
-        w_start(1, dg)
+
+    def emb_middle():
         for i in range(1, nz):
             t = (z + i) % nz
             arrived(eslot(e_y + t * n_pipe, n_pipe), ez_r.at[t])
         send_y.start()
-        w_on(1, dg)
+
+    def emb_end():
         arrived(eslot((c * 2 + 1 - y) * nz * n_pipe, nz * n_pipe), ey_r)
         send_c.start()
         for i in range(1, n_pipe):
             send_x(i).start()
-        w_here(0, ug)
-        arrived(eslot(oc * many, many), ec_r)
+
+    lx = (xl, xl_s, xl_r)
+    gx = (xg, x_s, x_r)
 
     @pl.when(p != last)
     def _():
-        w_on(1, dg)
-        w_here(0, ug)
+        send_a.start()
+
+    @pl.when(p == 0)
+    def _():
+        h_over(0, ul).start()
+        h_start(0, ul)
+        h_over(1, dl).start()
+        h_start(1, dl)
+        for m in range(micros):
+            tokens_out(*lx, m)
+        h_on(0, ul)
+        h_on(1, dl)
+
+    @pl.when(p == 1)
+    def _():
+        for m in range(micros):
+            tokens_out(*lx, m)
+        arrived(hslot(ul, q), hx_r.at[0])
+        h_start(0, ul)
+        arrived(hslot(dl, q), hx_r.at[1])
+        h_start(1, dl)
+        h_on(0, ul)
+        h_on(1, dl)
+
+    @pl.when(p <= 1)
+    def _():
+        tokens_on(*lx)
+
+    @pl.when(p > 0)
+    def _():
+        w_start(0, ug)
+
+    @pl.when(p == last)
+    def _():
+        emb_start()
 
     if spill:
         ids_all, tids_all = ids_ref, tids_ref
@@ -243,14 +295,10 @@
     per = tile // rows
     mt = per // 2
 
-    def activate(b, j):
-        values = xg[b, pl.ds(j * mt, mt)].reshape(tile, width).astype(F32)
-        act = jax.nn.gelu(dot(layer_norm(values), ug[...], NT), approximate=True)
+    def activate(buf, u, b, j):
+        values = buf[b, pl.ds(j * mt, mt)].reshape(tile, width).astype(F32)
+        act = jax.nn.gelu(dot(layer_norm(values), u[...], NT), approximate=True)
         return values, act.astype(BF16)
-
-    def hidden_out(m):
-        return copy(sz.at[1, m], xg.at[zb, m, c], h_s.at[m], h_r.at[m],
-                    jnp.minimum(p + 1, last), d)
 
     def to_core(b, m):
         return copy(sc.at[b, m], rc.at[b, m], c_s.at[b, m], c_r.at[b, m], p, d_c)
@@ -258,55 +306,124 @@
     def to_z(m):
         return copy(sz.at[0, m], rz.at[m], z_s.at[m], z_r.at[m], p, d_z)
 
-    def take_hidden():
-        for m in range(micros):
-            arrived(xg.at[zb, m, c], h_r.at[m])
-            x_c(m).start()
-            x_z(m).start()
-        tokens_on()
-
-    @pl.when((p > 0) & (p < last))
-    def _():
-        take_hidden()
-
-    @pl.when(p < last)
-    def _():
-        tokens_here()
-        if tiles > 1:
-            w_here(1, dg)
-        for b in (oz, zb):
-            def step(j, _, b=b):
-                _, act = activate(b, j)
-                if b is oz and tiles == 1:
-                    w_here(1, dg)
-                out = dot(act, dg[...], NN)
-                part[b, pl.ds(j * mt, mt)] = out.reshape(mt, 2, rows, width)
+    def reduce_rows(buf, u, dn, await_dn, between, emit):
+        for first, b in ((True, oz), (False, zb)):
+            def step(j, _, first=first, b=b):
+                _, act = activate(buf, u, b, j)
+                if first and tiles == 1:
+                    await_dn()
+                part[b, pl.ds(j * mt, mt)] = dot(act, dn[...], NN).reshape(mt, 2, rows, width)
                 return 0
 
             if tiles == 1:
                 step(0, 0)
             else:
+                if first:
+                    await_dn()
                 lax.fori_loop(0, tiles, step, 0)
             for m in range(micros):
                 sc[b, m] = part[b, m, oc].astype(BF16)
                 to_core(b, m).start()
-            if b is oz:
+            if first:
                 for m in range(micros):
                     arrived(rc.at[oz, m], c_r.at[oz, m])
                     sz[0, m] = (part[oz, m, c] + rc[oz, m].astype(F32)).astype(BF16)
                     to_z(m).start()
+        between()
         for m in range(micros):
             arrived(rc.at[zb, m], c_r.at[zb, m])
             arrived(rz.at[m], z_r.at[m])
-            new = part[zb, m, c] + rc[zb, m].astype(F32) + rz[m].astype(F32)
-            sz[1, m] = (new + xg[zb, m, c].astype(F32)).astype(BF16)
-            hidden_out(m).start()
+            emit(m, part[zb, m, c] + rc[zb, m].astype(F32) + rz[m].astype(F32))
         for m in range(micros):
             for b in range(2):
                 left(sc.at[b, m], c_s.at[b, m])
             left(sz.at[0, m], z_s.at[m])
+
+    def to_rx(m):
+        return copy(sz.at[1, m], rx.at[m], h_s.at[m], h_r.at[m], 1, d)
+
+    def hidden_out(m):
+        return copy(sz.at[1, m], xg.at[zb, m, c], h_s.at[m], h_r.at[m],
+                    jnp.minimum(p + 1, last), d)
+
+    @pl.when(p <= 1)
+    def _():
+        h_here(0, ul)
+        tokens_here(xl, xl_r)
+
+        def await_dl():
+            h_here(1, dl)
+
+        def between():
+            @pl.when(p == 1)
+            def _():
+                w_on(0, ug)
+                w_start(1, dg)
+
+            @pl.when(p == last)
+            def _():
+                emb_middle()
+
+        def emit(m, value):
+            @pl.when(p == 0)
+            def _():
+                sz[1, m] = value.astype(BF16)
+                to_rx(m).start()
+
+            @pl.when(p == 1)
+            def _():
+                arrived(rx.at[m], h_r.at[m])
+                new = value + rx[m].astype(F32) + xl[zb, m, c].astype(F32)
+                xg[zb, m, c] = new.astype(BF16)
+                tokens_out(*gx, m)
+
+        reduce_rows(xl, ul, dl, await_dl, between, emit)
+
+    def take_hidden():
+        for m in range(micros):
+            arrived(xg.at[zb, m, c], h_r.at[m])
+            tokens_out(*gx, m)
+
+    if n_pipe > 2:
+        @pl.when(p > 1)
+        def _():
+            w_start(1, dg)
+            w_on(0, ug)
+
+        @pl.when((p > 0) & (p < last))
+        def _():
+            @pl.when(p > 1)
+            def _():
+                take_hidden()
+
+            tokens_on(*gx)
+            w_on(1, dg)
+            w_here(0, ug)
+            tokens_here(xg, x_r)
+
+            def emit(m, value):
+                sz[1, m] = (value + xg[zb, m, c].astype(F32)).astype(BF16)
+                hidden_out(m).start()
+
+            reduce_rows(xg, ug, dg, lambda: w_here(1, dg), lambda: None, emit)
+
+        @pl.when(p == last)
+        def _():
+            emb_middle()
+
+    @pl.when(p == last)
+    def _():
+        emb_end()
+        if n_pipe == 2:
+            tokens_on(*gx)
+        w_on(1, dg)
+        w_here(0, ug)
+        arrived(eslot(oc * many, many), ec_r)
+
+    @pl.when(p != last)
+    def _():
+        for m in range(micros):
             left(sz.at[1, m], h_s.at[m])
-
         arrived(eslot(e_c, many), ex_r)
         send_c.start()
         arrived(eslot(oc * many, many), ec_r)
@@ -359,13 +476,15 @@
     def _():
         def step(i, _):
             b, j = i // tiles, i % tiles
-            values, act = activate(b, j)
+            values, act = activate(xg, ug, b, j)
             ma[i] = jnp.mean(act.astype(F32).reshape(per, rows, -1), axis=1)
             mx[i] = jnp.mean(values.reshape(per, rows, width), axis=1)
             return 0
 
-        take_hidden()
-        tokens_here()
+        if n_pipe > 2:
+            take_hidden()
+            tokens_on(*gx)
+        tokens_here(xg, x_r)
         lax.fori_loop(0, 2 * tiles, step, 0)
         w_here(1, dg)
         for i in range(2 * tiles):
@@ -433,14 +552,33 @@
         g_row = late(0, 0.0)
     img_ref[0:1, :] = g_row[0:1]
 
-    for k, ref in big:
-        for i in range(nzp):
-            left(w_ref.at[k], w_s.at[k, i])
-        for i in range(1, nzp):
-            left(w_ref.at[k], w_s.at[k, nzp + i])
-    for m in range(micros):
-        for i in range(3):
-            left(xg.at[zb, m, c], x_s.at[i, m])
+    @pl.when(p > 0)
+    def _():
+        for k, ref in big:
+            for i in range(nzp):
+                left(w_ref.at[k, pl.ds(0, ff)], w_s.at[k, i])
+            for i in range(1, nzp):
+                left(w_ref.at[k, pl.ds(0, ff)], w_s.at[k, nzp + i])
+        for m in range(micros):
+            for i in range(3):
+                left(xg.at[zb, m, c], x_s.at[i, m])
+
+    @pl.when(p == 0)
+    def _():
+        for k in range(2):
+            left(w_ref.at[k, pl.ds(half, half)], hx_s.at[k])
+
+    @pl.when(p <= 1)
+    def _():
+        for k, ref in halves:
+            for i in range(nzp):
+                left(hslot(ref, q), hw_s.at[k, i])
+            for i in range(1, nzp):
+                left(hslot(ref, q), hw_s.at[k, nzp + i])
+        for m in range(micros):
+            for i in range(3):
+                left(xl.at[zb, m, c], xl_s.at[i, m])
+
     send_c.wait_send()
 
     @pl.when(p == last)
@@ -495,6 +633,7 @@
     tiles, kept = span // tile, tile // rows
     imgs = 4 * micros
     ffg = groups * ff
+    half = -(-ff // 32) * 16
     vm = pl.BlockSpec(memory_space=pltpu.VMEM)
     sm = pl.BlockSpec(memory_space=pltpu.SMEM)
     dma = pltpu.SemaphoreType.DMA
@@ -504,7 +643,11 @@
     scratch = [
         pltpu.VMEM((SLOT, width), BF16),
         pltpu.VMEM((1024, width) if spill else (16, width), BF16),
-        pltpu.VMEM((2, ff, width), BF16),
+        pltpu.VMEM((2, 2 * half, width), BF16),
+        pltpu.VMEM((groups * half, width), BF16),
+        pltpu.VMEM((groups * half, width), BF16),
+        pltpu.VMEM((2, micros, 2, rows, width), BF16),
+        pltpu.VMEM((micros, rows, width), BF16),
         pltpu.VMEM((ffg, width), BF16),
         pltpu.VMEM((ffg, width), BF16),
         pltpu.VMEM((2, micros, 2, rows, width), BF16),
@@ -531,6 +674,9 @@
         dma, dma,
         dma((n_pipe,)), dma,
         dma, dma,
+        dma((2, 2 * nzp)), dma((2, groups)),
+        dma((2,)), dma((2,)),
+        dma((3, micros)), dma((2, micros, 2)),
         dma((2,)),
     ]
     if spill:

time: 99.1 us -> 123 us (1.24)
  Pallas kernels: 93.5 us -> 117 us
    pallas_call x1, Pallas kernels: 93.5 us -> 117 us  [body(): pl.pallas_call(functools.partial(kernel, cfg), out_shape=outs, in_specs=[...]
where the time goes in v3:
time: 123 us; the launch traced here: 122 us
  Pallas kernels  117 us (95%)
  local copies, waits for them, and re-layouts  3.43 us (3%)
  between operations  1.95 us (2%)
    pallas_call x1, Pallas kernels, body(): pl.pallas_call(functools.partial(kernel, cfg), out_shape=outs, in_specs=[...  117 us
    unnamed x6, local copies, waits for them, and re-layouts  2.87 us

profile of v3, /device:TPU:1, one launch (start us, length us, event | category | flops | bytes accessed | tf_op | source)
XLA Modules:
  0.0 122.3 jit_solution(1267293453193949147)
XLA Ops:
  1.9 0.0 copy-start.1
  1.9 0.7 copy-done.1
  2.6 0.6 reshape.10.ids_ref.tids_ref
  3.2 116.9 %shard_map.95 = (f32[9,1152]{1,0:T(8,128)}, f32[9,1152]{1,0:T(8,128)}) custom-call(f32[1]{0:T(128)S(6)} %copy.12.scale_ref, f32[1]{0:T(128)S(6)} %copy.13.shift_ref, s32[1,288]{1,0:T(1,128)} %reshape.10.ids_ref.tids_ref, s32[1,288]{1,0:T(1,128)} %reshape.10.ids_ref.tids_ref, bf16[2,64,1152]{2,1,0:T(8,128)(2,1)} %bitcast.7, bf16[136,1152]{1,0:T(8,128)(2,1)} %bitcast.5, ...), custom_call_target="tpu_custom_call" | custom-call | tf_op jit(solution)/shard_map/pallas_call | solution.py:687
  120.1 0.0 copy-start
  120.1 1.6 %copy.14 = f32[9,1152]{1,0:T(8,128)} copy(f32[9,1152]{1,0:T(8,128)} %get-tuple-element.4) | data formatting | bytes 82944
  121.7 0.0 copy-done
  121.7 0.6 copy.15
Async XLA Ops:
  1.9 0.7 copy-start.1
  120.1 1.6 %copy-start = (f32[9,1152]{1,0:T(8,128)S(1)}, f32[9,1152]{1,0:T(8,128)}, u32[]{:S(2)}) copy-start(f32[9,1152]{1,0:T(8,128)} %get-tuple-element.5) | copy-start | bytes 124420

commit v4 on v3

--- a/solution.py
+++ b/solution.py
@@ -41,6 +41,7 @@
     else:
         *rest, eg = rest
     (own, chunk, w_ref, ul, dl, xl, rx, ug, dg, xg, part, sc, rc, sz, rz, ma, ma2, mx, mx2, tp, tall,
+     mq, rq, pq, bq, mq_s, mq_r, pq_s, pq_r,
      w_s, w_r, x_s, x_r, c_s, c_r, z_s, z_r, h_s, h_r, tp_s, tp_r, ta_s, ta_r,
      ea_s, ea_r, ez_s, ez_r, ey_s, ey_r, ex_s, ex_r, ec_s, ec_r,
      hw_s, hw_r, hx_s, hx_r, xl_s, xl_r, loc) = rest
@@ -358,7 +359,8 @@
             @pl.when(p == 1)
             def _():
                 w_on(0, ug)
-                w_start(1, dg)
+                if n_pipe > 2:
+                    w_start(1, dg)
 
             @pl.when(p == last)
             def _():
@@ -387,7 +389,10 @@
     if n_pipe > 2:
         @pl.when(p > 1)
         def _():
-            w_start(1, dg)
+            @pl.when(p < last)
+            def _():
+                w_start(1, dg)
+
             w_on(0, ug)
 
         @pl.when((p > 0) & (p < last))
@@ -416,7 +421,6 @@
         emb_end()
         if n_pipe == 2:
             tokens_on(*gx)
-        w_on(1, dg)
         w_here(0, ug)
         arrived(eslot(oc * many, many), ec_r)
 
@@ -486,12 +490,36 @@
             tokens_on(*gx)
         tokens_here(xg, x_r)
         lax.fori_loop(0, 2 * tiles, step, 0)
-        w_here(1, dg)
         for i in range(2 * tiles):
             ma2[i * per:(i + 1) * per, :] = ma[i]
             mx2[i * per:(i + 1) * per, :] = mx[i]
         t = zb * 2 + c
-        tp[t] = dot(ma2[...].astype(BF16), dg[...], NN)
+        for g in range(groups):
+            mq[g] = ma2[:, g * ff:(g + 1) * ff]
+        rq[q] = mq[q]
+
+        def across(src, dst, ss, rr, i):
+            g = (q + i) % groups
+            return copy(src.at[g], dst.at[q], ss.at[i], rr.at[q], p,
+                        at((g // 2) * 2 + zb, g % 2, c))
+
+        for i in range(1, groups):
+            across(mq, rq, mq_s, mq_r, i).start()
+        for i in range(1, groups):
+            g = (q + i) % groups
+            arrived(rq.at[g], mq_r.at[g])
+        means = rq[...].reshape(groups * rq.shape[1], ff).astype(BF16)
+        pq[...] = dot(means, w_ref[1, 0:ff, :], NN).reshape(pq.shape)
+        bq[q] = pq[q]
+        for i in range(1, groups):
+            across(pq, bq, pq_s, pq_r, i).start()
+        for i in range(1, groups):
+            g = (q + i) % groups
+            arrived(bq.at[g], pq_r.at[g])
+        tp[t] = jnp.sum(bq[...], axis=0)
+        for i in range(1, groups):
+            left(mq.at[q], mq_s.at[i])
+            left(pq.at[q], pq_s.at[i])
 
         def t_out(i):
             t_ = (t + i) % 4
@@ -554,11 +582,15 @@
 
     @pl.when(p > 0)
     def _():
-        for k, ref in big:
+        def gone(k):
             for i in range(nzp):
                 left(w_ref.at[k, pl.ds(0, ff)], w_s.at[k, i])
             for i in range(1, nzp):
                 left(w_ref.at[k, pl.ds(0, ff)], w_s.at[k, nzp + i])
+
+        gone(0)
+        if n_pipe > 2:
+            pl.when(p < last)(lambda: gone(1))
         for m in range(micros):
             for i in range(3):
                 left(xg.at[zb, m, c], x_s.at[i, m])
@@ -662,6 +694,11 @@
         pltpu.VMEM((imgs, width), F32),
         pltpu.VMEM((4, imgs, width), F32),
         pltpu.VMEM((groups, imgs, width), F32),
+        pltpu.VMEM((groups, imgs, ff), F32),
+        pltpu.VMEM((groups, imgs, ff), F32),
+        pltpu.VMEM((groups, imgs, width), F32),
+        pltpu.VMEM((groups, imgs, width), F32),
+        dma((groups,)), dma((groups,)), dma((groups,)), dma((groups,)),
         dma((2, 2 * nzp)), dma((2, groups)),
         dma((3, micros)), dma((2, micros, 2)),
         dma((2, micros)), dma((2, micros)),

time: 123 us -> 116 us (0.943)
  Pallas kernels: 117 us -> 110 us
    pallas_call x1, Pallas kernels: 117 us -> 110 us  [body(): pl.pallas_call(functools.partial(kernel, cfg), out_shape=outs, in_specs=[...]
where the time goes in v4:
time: 116 us; the launch traced here: 115 us
  Pallas kernels  110 us (95%)
  local copies, waits for them, and re-layouts  3.43 us (3%)
  between operations  1.95 us (2%)
    pallas_call x1, Pallas kernels, body(): pl.pallas_call(functools.partial(kernel, cfg), out_shape=outs, in_specs=[...  110 us
    unnamed x6, local copies, waits for them, and re-layouts  2.87 us

profile of v4, /device:TPU:1, one launch (start us, length us, event | category | flops | bytes accessed | tf_op | source)
XLA Modules:
  0.0 115.3 jit_solution(16572668172679051448)
XLA Ops:
  1.9 0.0 copy-start.1
  1.9 0.7 copy-done.1
  2.6 0.6 reshape.10.ids_ref.tids_ref
  3.2 109.9 %shard_map.95 = (f32[9,1152]{1,0:T(8,128)}, f32[9,1152]{1,0:T(8,128)}) custom-call(f32[1]{0:T(128)S(6)} %copy.12.scale_ref, f32[1]{0:T(128)S(6)} %copy.13.shift_ref, s32[1,288]{1,0:T(1,128)} %reshape.10.ids_ref.tids_ref, s32[1,288]{1,0:T(1,128)} %reshape.10.ids_ref.tids_ref, bf16[2,64,1152]{2,1,0:T(8,128)(2,1)} %bitcast.7, bf16[136,1152]{1,0:T(8,128)(2,1)} %bitcast.5, ...), custom_call_target="tpu_custom_call" | custom-call | tf_op jit(solution)/shard_map/pallas_call | solution.py:724
  113.1 0.0 copy-start
  113.1 1.6 %copy.14 = f32[9,1152]{1,0:T(8,128)} copy(f32[9,1152]{1,0:T(8,128)} %get-tuple-element.4) | data formatting | bytes 82944
  114.7 0.0 copy-done
  114.7 0.6 copy.15
Async XLA Ops:
  1.9 0.7 copy-start.1
  113.1 1.6 %copy-start = (f32[9,1152]{1,0:T(8,128)S(1)}, f32[9,1152]{1,0:T(8,128)}, u32[]{:S(2)}) copy-start(f32[9,1152]{1,0:T(8,128)} %get-tuple-element.5) | copy-start | bytes 124420

commit v5 on v2

--- a/solution.py
+++ b/solution.py
@@ -41,6 +41,7 @@
     else:
         *rest, eg = rest
     (own, chunk, w_ref, ug, dg, xg, part, sc, rc, sz, rz, ma, ma2, mx, mx2, tp, tall,
+     mq, rq, pq, bq, mq_s, mq_r, pq_s, pq_r,
      w_s, w_r, x_s, x_r, c_s, c_r, z_s, z_r, h_s, h_r, tp_s, tp_r, ta_s, ta_r,
      ea_s, ea_r, ez_s, ez_r, ey_s, ey_r, ex_s, ex_r, ec_s, ec_r, loc) = rest
     p, d = lax.axis_index("pipe"), lax.axis_index("dp")
@@ -194,12 +195,10 @@
         for i in range(1, nz):
             send_z(i).start()
         w_on(0, ug)
-        w_start(1, dg)
         for i in range(1, nz):
             t = (z + i) % nz
             arrived(eslot(e_y + t * n_pipe, n_pipe), ez_r.at[t])
         send_y.start()
-        w_on(1, dg)
         arrived(eslot((c * 2 + 1 - y) * nz * n_pipe, nz * n_pipe), ey_r)
         send_c.start()
         for i in range(1, n_pipe):
@@ -367,12 +366,36 @@
         take_hidden()
         tokens_here()
         lax.fori_loop(0, 2 * tiles, step, 0)
-        w_here(1, dg)
         for i in range(2 * tiles):
             ma2[i * per:(i + 1) * per, :] = ma[i]
             mx2[i * per:(i + 1) * per, :] = mx[i]
         t = zb * 2 + c
-        tp[t] = dot(ma2[...].astype(BF16), dg[...], NN)
+        for g in range(groups):
+            mq[g] = ma2[:, g * ff:(g + 1) * ff]
+        rq[q] = mq[q]
+
+        def across(src, dst, ss, rr, i):
+            g = (q + i) % groups
+            return copy(src.at[g], dst.at[q], ss.at[i], rr.at[q], p,
+                        at((g // 2) * 2 + zb, g % 2, c))
+
+        for i in range(1, groups):
+            across(mq, rq, mq_s, mq_r, i).start()
+        for i in range(1, groups):
+            g = (q + i) % groups
+            arrived(rq.at[g], mq_r.at[g])
+        means = rq[...].reshape(groups * rq.shape[1], ff).astype(BF16)
+        pq[...] = dot(means, w_ref[1, 0:ff, :], NN).reshape(pq.shape)
+        bq[q] = pq[q]
+        for i in range(1, groups):
+            across(pq, bq, pq_s, pq_r, i).start()
+        for i in range(1, groups):
+            g = (q + i) % groups
+            arrived(bq.at[g], pq_r.at[g])
+        tp[t] = jnp.sum(bq[...], axis=0)
+        for i in range(1, groups):
+            left(mq.at[q], mq_s.at[i])
+            left(pq.at[q], pq_s.at[i])
 
         def t_out(i):
             t_ = (t + i) % 4
@@ -433,11 +456,14 @@
         g_row = late(0, 0.0)
     img_ref[0:1, :] = g_row[0:1]
 
-    for k, ref in big:
+    def gone(k):
         for i in range(nzp):
             left(w_ref.at[k], w_s.at[k, i])
         for i in range(1, nzp):
             left(w_ref.at[k], w_s.at[k, nzp + i])
+
+    gone(0)
+    pl.when(p < last)(lambda: gone(1))
     for m in range(micros):
         for i in range(3):
             left(xg.at[zb, m, c], x_s.at[i, m])
@@ -519,6 +545,11 @@
         pltpu.VMEM((imgs, width), F32),
         pltpu.VMEM((4, imgs, width), F32),
         pltpu.VMEM((groups, imgs, width), F32),
+        pltpu.VMEM((groups, imgs, ff), F32),
+        pltpu.VMEM((groups, imgs, ff), F32),
+        pltpu.VMEM((groups, imgs, width), F32),
+        pltpu.VMEM((groups, imgs, width), F32),
+        dma((groups,)), dma((groups,)), dma((groups,)), dma((groups,)),
         dma((2, 2 * nzp)), dma((2, groups)),
         dma((3, micros)), dma((2, micros, 2)),
         dma((2, micros)), dma((2, micros)),

time: 99.1 us -> 97.2 us (0.981)
  Pallas kernels: 93.5 us -> 91.3 us
    pallas_call x1, Pallas kernels: 93.5 us -> 91.3 us  [body(): pl.pallas_call(functools.partial(kernel, cfg), out_shape=outs, in_specs=[...]
where the time goes in v5:
time: 97.2 us; the launch traced here: 96.6 us
  Pallas kernels  91.3 us (94%)
  local copies, waits for them, and re-layouts  3.43 us (4%)
  between operations  1.95 us (2%)
    pallas_call x1, Pallas kernels, body(): pl.pallas_call(functools.partial(kernel, cfg), out_shape=outs, in_specs=[...  91.3 us
    unnamed x6, local copies, waits for them, and re-layouts  2.87 us

profile of v5, /device:TPU:1, one launch (start us, length us, event | category | flops | bytes accessed | tf_op | source)
XLA Modules:
  0.0 96.6 jit_solution(7061648447715028154)
XLA Ops:
  1.9 0.0 copy-start.1
  1.9 0.7 copy-done.1
  2.6 0.6 reshape.10.ids_ref.tids_ref
  3.2 91.3 %shard_map.95 = (f32[9,1152]{1,0:T(8,128)}, f32[9,1152]{1,0:T(8,128)}) custom-call(f32[1]{0:T(128)S(6)} %copy.12.scale_ref, f32[1]{0:T(128)S(6)} %copy.13.shift_ref, s32[1,288]{1,0:T(1,128)} %reshape.10.ids_ref.tids_ref, s32[1,288]{1,0:T(1,128)} %reshape.10.ids_ref.tids_ref, bf16[2,64,1152]{2,1,0:T(8,128)(2,1)} %bitcast.7, bf16[136,1152]{1,0:T(8,128)(2,1)} %bitcast.5, ...), custom_call_target="tpu_custom_call" | custom-call | tf_op jit(solution)/shard_map/pallas_call | solution.py:572
  94.4 0.0 copy-start
  94.5 1.6 %copy.14 = f32[9,1152]{1,0:T(8,128)} copy(f32[9,1152]{1,0:T(8,128)} %get-tuple-element.4) | data formatting | bytes 82944
  96.0 0.0 copy-done
  96.0 0.6 copy.15
Async XLA Ops:
  1.9 0.7 copy-start.1
  94.4 1.6 %copy-start = (f32[9,1152]{1,0:T(8,128)S(1)}, f32[9,1152]{1,0:T(8,128)}, u32[]{:S(2)}) copy-start(f32[9,1152]{1,0:T(8,128)} %get-tuple-element.5) | copy-start | bytes 124420

commit v6 on v5

--- a/solution.py
+++ b/solution.py
@@ -178,8 +178,8 @@
     @pl.when(p != last)
     def _():
         send_a.start()
+        w_on(0, ug)
         w_start(1, dg)
-        w_on(0, ug)
 
     @pl.when(p == 0)
     def _():

time: 97.2 us -> 97.2 us (level)
  no operation moved by 1% of the time
where the time goes in v6:
time: 97.2 us; the launch traced here: 96.6 us
  Pallas kernels  91.3 us (94%)
  local copies, waits for them, and re-layouts  3.43 us (4%)
  between operations  1.95 us (2%)
    pallas_call x1, Pallas kernels, body(): pl.pallas_call(functools.partial(kernel, cfg), out_shape=outs, in_specs=[...  91.3 us
    unnamed x6, local copies, waits for them, and re-layouts  2.87 us

profile of v6, /device:TPU:1, one launch (start us, length us, event | category | flops | bytes accessed | tf_op | source)
XLA Modules:
  0.0 96.6 jit_solution(10169428204762442045)
XLA Ops:
  1.9 0.0 copy-start.1
  1.9 0.7 copy-done.1
  2.6 0.6 reshape.10.ids_ref.tids_ref
  3.2 91.3 %shard_map.95 = (f32[9,1152]{1,0:T(8,128)}, f32[9,1152]{1,0:T(8,128)}) custom-call(f32[1]{0:T(128)S(6)} %copy.12.scale_ref, f32[1]{0:T(128)S(6)} %copy.13.shift_ref, s32[1,288]{1,0:T(1,128)} %reshape.10.ids_ref.tids_ref, s32[1,288]{1,0:T(1,128)} %reshape.10.ids_ref.tids_ref, bf16[2,64,1152]{2,1,0:T(8,128)(2,1)} %bitcast.7, bf16[136,1152]{1,0:T(8,128)(2,1)} %bitcast.5, ...), custom_call_target="tpu_custom_call" | custom-call | tf_op jit(solution)/shard_map/pallas_call | solution.py:572
  94.4 0.0 copy-start
  94.5 1.6 %copy.14 = f32[9,1152]{1,0:T(8,128)} copy(f32[9,1152]{1,0:T(8,128)} %get-tuple-element.4) | data formatting | bytes 82944
  96.0 0.0 copy-done
  96.0 0.6 copy.15
Async XLA Ops:
  1.9 0.7 copy-start.1
  94.4 1.6 %copy-start = (f32[9,1152]{1,0:T(8,128)S(1)}, f32[9,1152]{1,0:T(8,128)}, u32[]{:S(2)}) copy-start(f32[9,1152]{1,0:T(8,128)} %get-tuple-element.5) | copy-start | bytes 124420
